TPU v7x, 32 devices: a whole 2x2x4 slice. The times are simulated.
32 devices in a mesh: shard: 4 (over y, x), context: 4 (over z), tensor: 2 (over core).
Axes of the slice: x: 2, y: 2, z: 4, core: 2. Of those that a mesh axis runs over, the one named last changes fastest.
Arguments:
- inputs: bfloat16 [64, 512, 1024], P('shard', 'context'), may hold values from -6 to 6
- lengths: int32 [64], P('shard'), may hold values from 1 to 512, as said below
- w_qkv: bfloat16 [3, 1024, 1024], P(None, ('shard', 'context'), 'tensor'), may hold values from -0.1875 to 0.1875
- b_qv: float32 [2, 1024], P(None, 'tensor'), may hold values from -1.5 to 1.5
- w_out: bfloat16 [1024, 1024], P('tensor', ('shard', 'context')), may hold values from -1 to 1
- b_out: float32 [1024], replicated, may hold values from -1.5 to 1.5
- w_up: bfloat16 [1024, 4096], P(('shard', 'context'), 'tensor'), may hold values from -0.1875 to 0.1875
- b_up: float32 [4096], P('tensor'), may hold values from -1.5 to 1.5
- w_down: bfloat16 [4096, 1024], P('tensor', ('shard', 'context')), may hold values from -0.09375 to 0.09375
- down_bias: float32 [1024], replicated, may hold values from -1.5 to 1.5
- gain_attn: float32 [1024], replicated, may hold values from 0.1 to 1.9
- shift_attn: float32 [1024], replicated, may hold values from -1.5 to 1.5
- gain_ffn: float32 [1024], replicated, may hold values from 0.1 to 1.9
- shift_ffn: float32 [1024], replicated, may hold values from -1.5 to 1.5
- grad_output: bfloat16 [64, 512, 1024], P('shard', 'context'), may hold values from -6 to 6
Outputs:
- outputs: bfloat16 [64, 512, 1024], P('shard', 'context')
- grad_inputs: bfloat16 [64, 512, 1024], P('shard', 'context')
- grad_w_qkv: float32 [3, 1024, 1024], P(None, ('shard', 'context'), 'tensor')
- grad_b_qv: float32 [2, 1024], P(None, 'tensor')
- grad_w_out: float32 [1024, 1024], P('tensor', ('shard', 'context'))
- grad_b_out: float32 [1024], replicated
- grad_w_up: float32 [1024, 4096], P(('shard', 'context'), 'tensor')
- up_bias_gradient: float32 [4096], P('tensor')
- grad_w_down: float32 [4096, 1024], P('tensor', ('shard', 'context'))
- grad_b_down: float32 [1024], replicated
- grad_gain_attn: float32 [1024], replicated
- grad_shift_attn: float32 [1024], replicated
- grad_gain_ffn: float32 [1024], replicated
- grad_shift_ffn: float32 [1024], replicated
Inputs may be any that keep to these rules, and one draw needn't show every extreme that they name: In every group of 16 sequences along the shard axis, one has length 512; group lengths differ in their lower range.
All inputs are finite; a program needn't handle non-finite values.
Results may differ from a plain program's by a relative error of at most 0.02.
Values may be sent and summed in bfloat16 or wider, within the bound.
A program may use at most 192 MiB of HBM per device.

v0:
```python
import jax
import jax.numpy as jnp
from jax import lax
from jax.sharding import PartitionSpec as P

HEAD_DIM = 64


NEG_FILL = -1000000000.0
EPSILON = 1e-12


def layer_norm(resid, gain, shift):
    center = resid - jnp.mean(resid, -1, keepdims=True)
    spread = jnp.mean(center * center, -1, keepdims=True)
    return center * lax.rsqrt(spread + EPSILON) * gain + shift


def gelu_exact(values_in):
    return jax.nn.gelu(values_in, approximate=False)


def matmul_nt(left_operand, right):
    return lax.dot_general(
        left_operand, right, (((1,), (1,)), ((), ())), preferred_element_type=jnp.float32
    )


def matmul_tn(left_operand, right):
    return lax.dot_general(
        left_operand, right, (((0,), (0,)), ((), ())), preferred_element_type=jnp.float32
    )


def head_scores(query, key_rows, length_value):
    count = query.shape[0]
    heads_here = query.shape[1] // HEAD_DIM
    q_three = query.reshape(count, heads_here, HEAD_DIM)
    k_three = key_rows.reshape(count, heads_here, HEAD_DIM)
    scores = jnp.einsum(
        "qhd,khd->hqk", q_three, k_three, preferred_element_type=jnp.float32
    ) * HEAD_DIM ** (-0.5)
    usable = jnp.arange(count, dtype=jnp.int32) < length_value
    return (jnp.where(usable[None, None, :], scores, NEG_FILL), q_three, k_three)


def attend_forward(sliced):
    query, key_rows, value_rows, length_value = sliced
    scores, q_three, k_three = head_scores(query, key_rows, length_value)
    v_three = value_rows.reshape(k_three.shape)
    top_score = jnp.max(scores, -1, keepdims=True)
    weights = jnp.exp(scores - top_score)
    denom = jnp.sum(weights, -1, keepdims=True)
    probs = (weights / denom).astype(jnp.bfloat16)
    result = jnp.einsum("hqk,khd->qhd", probs, v_three, preferred_element_type=jnp.float32)
    log_total = (top_score + jnp.log(denom))[..., 0]
    return (result.reshape(query.shape).astype(jnp.bfloat16), log_total)


def attend_backward(sliced):
    query, key_rows, value_rows, log_total, grad_attn, length_value = sliced
    scores, q_three, k_three = head_scores(query, key_rows, length_value)
    v_three = value_rows.reshape(k_three.shape)
    g_three = grad_attn.reshape(k_three.shape)
    probs_full = jnp.exp(scores - log_total[..., None])
    probs = probs_full.astype(jnp.bfloat16)
    grad_value = jnp.einsum("hqk,qhd->khd", probs, g_three, preferred_element_type=jnp.float32)
    grad_probs = jnp.einsum("qhd,khd->hqk", g_three, v_three, preferred_element_type=jnp.float32)
    centered = grad_probs - jnp.sum(probs_full * grad_probs, -1, keepdims=True)
    grad_scores = (probs_full * centered).astype(jnp.bfloat16)
    scale = HEAD_DIM ** (-0.5)
    grad_query = (
        jnp.einsum("hqk,khd->qhd", grad_scores, k_three, preferred_element_type=jnp.float32) * scale
    )
    grad_key = (
        jnp.einsum("hqk,qhd->khd", grad_scores, q_three, preferred_element_type=jnp.float32) * scale
    )
    shape_out = query.shape
    return (
        grad_query.reshape(shape_out).astype(jnp.bfloat16),
        grad_key.reshape(shape_out).astype(jnp.bfloat16),
        grad_value.reshape(shape_out).astype(jnp.bfloat16),
    )


def on_device(
    inputs,
    lengths,
    w_qkv,
    b_qv,
    w_out,
    b_out,
    w_up,
    b_up,
    w_down,
    down_bias,
    gain_attn,
    shift_attn,
    gain_ffn,
    shift_ffn,
    grad_output,
):
    seq_count, piece_len, model_width = inputs.shape
    row_count = seq_count * piece_len
    full_qkv, full_out, full_up, full_down = (
        lax.all_gather(w_qkv, ("shard", "context"), axis=1, tiled=True),
        lax.all_gather(w_out, ("shard", "context"), axis=1, tiled=True),
        lax.all_gather(w_up, ("shard", "context"), axis=0, tiled=True),
        lax.all_gather(w_down, ("shard", "context"), axis=1, tiled=True),
    )
    flat_in = inputs.reshape(row_count, model_width)
    head_cols = full_qkv.shape[2]
    query = (jnp.dot(flat_in, full_qkv[0], preferred_element_type=jnp.float32) + b_qv[0]).astype(
        jnp.bfloat16
    )
    key_rows = jnp.dot(flat_in, full_qkv[1], preferred_element_type=jnp.float32).astype(
        jnp.bfloat16
    )
    value_rows = (
        jnp.dot(flat_in, full_qkv[2], preferred_element_type=jnp.float32) + b_qv[1]
    ).astype(jnp.bfloat16)
    piece_shape = (seq_count, piece_len, head_cols)
    head_query, head_key, head_value = (
        lax.all_to_all(
            query.reshape(piece_shape), "context", split_axis=2, concat_axis=1, tiled=True
        ),
        lax.all_to_all(
            key_rows.reshape(piece_shape), "context", split_axis=2, concat_axis=1, tiled=True
        ),
        lax.all_to_all(
            value_rows.reshape(piece_shape), "context", split_axis=2, concat_axis=1, tiled=True
        ),
    )
    head_attn, log_total = lax.map(attend_forward, (head_query, head_key, head_value, lengths))
    attn = lax.all_to_all(head_attn, "context", split_axis=1, concat_axis=2, tiled=True).reshape(
        row_count, head_cols
    )
    attn_part = jnp.dot(attn, full_out, preferred_element_type=jnp.float32)
    resid_attn = (
        inputs.astype(jnp.float32).reshape(row_count, model_width)
        + lax.psum(attn_part.astype(jnp.bfloat16), "tensor").astype(jnp.float32)
        + b_out
    )
    hidden = layer_norm(resid_attn, gain_attn, shift_attn)
    hidden_low = hidden.astype(jnp.bfloat16)
    pre_act = jnp.dot(hidden_low, full_up, preferred_element_type=jnp.float32) + b_up
    activ = gelu_exact(pre_act).astype(jnp.bfloat16)
    ffn_part = jnp.dot(activ, full_down, preferred_element_type=jnp.float32)
    resid_ffn = (
        hidden + lax.psum(ffn_part.astype(jnp.bfloat16), "tensor").astype(jnp.float32) + down_bias
    )
    outputs = layer_norm(resid_ffn, gain_ffn, shift_ffn)
    back_qkv, back_out, back_up, back_down = (
        lax.all_gather(w_qkv, ("shard", "context"), axis=1, tiled=True),
        lax.all_gather(w_out, ("shard", "context"), axis=1, tiled=True),
        lax.all_gather(w_up, ("shard", "context"), axis=0, tiled=True),
        lax.all_gather(w_down, ("shard", "context"), axis=1, tiled=True),
    )
    grad_flat = grad_output.astype(jnp.float32).reshape(row_count, model_width)
    outs_again, norm_pull = jax.vjp(layer_norm, resid_ffn, gain_ffn, shift_ffn)
    dresid_ffn, grad_gain_ffn, grad_shift_ffn = norm_pull(grad_flat)
    grad_b_down = jnp.sum(dresid_ffn, 0)
    dbranch_ffn = dresid_ffn.astype(jnp.bfloat16)
    grad_w_down = matmul_tn(activ, dbranch_ffn)
    dactiv = matmul_nt(dbranch_ffn, back_down)
    act_again, gelu_pull = jax.vjp(gelu_exact, pre_act)
    dpre_act = gelu_pull(dactiv)[0].astype(jnp.bfloat16)
    up_bias_gradient = jnp.sum(dpre_act.astype(jnp.float32), 0)
    grad_w_up = matmul_tn(hidden_low, dpre_act)
    hidden_part = matmul_nt(dpre_act, back_up)
    dhidden = dresid_ffn + lax.psum(hidden_part.astype(jnp.bfloat16), "tensor").astype(jnp.float32)
    hidden_again, attn_norm_pull = jax.vjp(layer_norm, resid_attn, gain_attn, shift_attn)
    dresid_attn, grad_gain_attn, grad_shift_attn = attn_norm_pull(dhidden)
    grad_b_out = jnp.sum(dresid_attn, 0)
    dbranch_attn = dresid_attn.astype(jnp.bfloat16)
    grad_w_out = matmul_tn(attn, dbranch_attn)
    dattn = matmul_nt(dbranch_attn, back_out).astype(jnp.bfloat16)
    head_dattn = lax.all_to_all(
        dattn.reshape(piece_shape), "context", split_axis=2, concat_axis=1, tiled=True
    )
    head_dquery, head_dkey, head_dvalue = lax.map(
        attend_backward, (head_query, head_key, head_value, log_total, head_dattn, lengths)
    )
    dquery, dkey, dvalue = (
        lax.all_to_all(head_dquery, "context", split_axis=1, concat_axis=2, tiled=True),
        lax.all_to_all(head_dkey, "context", split_axis=1, concat_axis=2, tiled=True),
        lax.all_to_all(head_dvalue, "context", split_axis=1, concat_axis=2, tiled=True),
    )
    dquery = dquery.reshape(row_count, head_cols)
    dkey = dkey.reshape(row_count, head_cols)
    dvalue = dvalue.reshape(row_count, head_cols)
    grad_b_qv = jnp.stack(
        [jnp.sum(dquery.astype(jnp.float32), 0), jnp.sum(dvalue.astype(jnp.float32), 0)]
    )
    grad_w_qkv = jnp.stack(
        [matmul_tn(flat_in, dquery), matmul_tn(flat_in, dkey), matmul_tn(flat_in, dvalue)]
    )
    input_part = (
        matmul_nt(dquery, back_qkv[0])
        + matmul_nt(dkey, back_qkv[1])
        + matmul_nt(dvalue, back_qkv[2])
    )
    grad_inputs = dresid_attn + lax.psum(input_part.astype(jnp.bfloat16), "tensor").astype(
        jnp.float32
    )
    shard_qkv, shard_out, shard_up, shard_down = (
        lax.psum_scatter(grad_w_qkv, ("shard", "context"), scatter_dimension=1, tiled=True),
        lax.psum_scatter(grad_w_out, ("shard", "context"), scatter_dimension=1, tiled=True),
        lax.psum_scatter(grad_w_up, ("shard", "context"), scatter_dimension=0, tiled=True),
        lax.psum_scatter(grad_w_down, ("shard", "context"), scatter_dimension=1, tiled=True),
    )
    small_sums = lax.psum(
        (
            grad_b_qv,
            grad_b_out,
            up_bias_gradient,
            grad_b_down,
            grad_gain_attn,
            grad_shift_attn,
            grad_gain_ffn,
            grad_shift_ffn,
        ),
        ("shard", "context"),
    )
    out_shape = (seq_count, piece_len, model_width)
    return (
        outputs.reshape(out_shape).astype(jnp.bfloat16),
        grad_inputs.reshape(out_shape).astype(jnp.bfloat16),
        shard_qkv,
        small_sums[0],
        shard_out,
        small_sums[1],
        shard_up,
        small_sums[2],
        shard_down,
        small_sums[3],
        small_sums[4],
        small_sums[5],
        small_sums[6],
        small_sums[7],
    )


def solution(mesh):
    placed = (
        P("shard", "context", None),
        P("shard"),
        P(None, ("shard", "context"), "tensor"),
        P(None, "tensor"),
        P("tensor", ("shard", "context")),
        P(),
        P(("shard", "context"), "tensor"),
        P("tensor"),
        P("tensor", ("shard", "context")),
        P(),
        P(),
        P(),
        P(),
        P(),
        P("shard", "context", None),
    )
    return jax.shard_map(
        on_device,
        mesh=mesh,
        in_specs=placed,
        out_specs=(
            P("shard", "context", None),
            P("shard", "context", None),
            P(None, ("shard", "context"), "tensor"),
            P(None, "tensor"),
            P("tensor", ("shard", "context")),
            P(),
            P(("shard", "context"), "tensor"),
            P("tensor"),
            P("tensor", ("shard", "context")),
            P(),
            P(),
            P(),
            P(),
            P(),
        ),
        check_vma=False,
    )
```

profile of v0, /device:TPU:0, one launch (start us, length us, event | category | flops | bytes accessed | tf_op | source)
XLA Modules:
  0.0 1910.3 jit_solution(12032369751570995187)
XLA Ops:
  8.7 72.6 %all-gather.5.cloned.1.call-done = bf16[3,1024,512]{2,1,0:T(8,128)(2,1)} async-done(((bf16[3,64,512]{2,1,0:T(8,128)(2,1)}), bf16[3,1024,512]{2,1,0:T(8,128)(2,1)}) %all-gather.5.cloned.1.call-update) | async-done | bytes 3145744 | tf_op jit(solution)/shard_map/all_gather | solution.py:106
  103.4 37.3 %all-to-all-done.1 = bf16[16,128,512]{1,0,2:T(8,128)(2,1)S(1)} async-done(((bf16[16,128,512]{1,0,2:T(8,128)(2,1)}), bf16[16,128,512]{1,0,2:T(8,128)(2,1)S(1)}, u32[]{:S(2)}, u32[]{:S(2)}) %all-to-all-start.1) | async-done | bytes 2097184 | tf_op jit(solution)/shard_map/all_to_all | solution.py:124
  155.8 37.1 %all-to-all-done = bf16[16,128,512]{1,0,2:T(8,128)(2,1)} async-done(((bf16[16,128,512]{1,0,2:T(8,128)(2,1)}), bf16[16,128,512]{1,0,2:T(8,128)(2,1)}, u32[]{:S(2)}, u32[]{:S(2)}) %all-to-all-start) | async-done | bytes 2097184 | tf_op jit(solution)/shard_map/all_to_all | solution.py:130
  210.4 35.2 %all-to-all-done.2 = bf16[16,128,512]{1,0,2:T(8,128)(2,1)} async-done(((bf16[16,128,512]{1,0,2:T(8,128)(2,1)}), bf16[16,128,512]{1,0,2:T(8,128)(2,1)}, u32[]{:S(2)}, u32[]{:S(2)}) %all-to-all-start.2) | async-done | bytes 2097184 | tf_op jit(solution)/shard_map/all_to_all | solution.py:127
  251.3 88.7 %while.26 = (s32[]{:T(128)}, bf16[16,512,128]{1,2,0:T(8,128)(2,1)S(1)}, f32[16,2,512]{2,1,0:T(2,128)}, bf16[16,512,128]{1,2,0:T(8,128)(2,1)}, s32[16]{0:T(128)S(...) while((s32[]{:T(128)}, bf16[16,512,128]{1,2,0:T(8,128)(2,1)S(1)}, ...), condition=%wide.region_3.4_spmd, body=%wide.region_0.3_spmd.sunk | while | flops 140574208 | bytes 7899761 | solution.py:134
  347.5 49.2 %all-to-all-done.3 = bf16[16,512,128]{2,0,1:T(8,128)(2,1)S(1)} async-done(((bf16[16,512,128]{2,0,1:T(8,128)(2,1)}), bf16[16,512,128]{2,0,1:T(8,128)(2,1)S(1)}, u32[]{:S(2)}, u32[]{:S(2)}) %all-to-all-start.3) | async-done | bytes 2097184 | tf_op jit(solution)/shard_map/all_to_all | solution.py:135
  400.4 21.2 %all-gather.7.cloned.1.call-done = bf16[512,1024]{0,1:T(8,128)(2,1)} async-done(((bf16[512,64]{0,1:T(8,128)(2,1)}), bf16[512,1024]{0,1:T(8,128)(2,1)}) %all-gather.7.cloned.1.call-update) | async-done | bytes 1048592 | tf_op jit(solution)/shard_map/all_gather | solution.py:107
  429.4 26.0 %all-reduce.8.cloned.1.call-done = bf16[2048,1024]{1,0:T(8,128)(2,1)} async-done(((bf16[2048,1024]{1,0:T(8,128)(2,1)}), bf16[2048,1024]{1,0:T(8,128)(2,1)}) %all-reduce.8.cloned.1.call-update) | async-done | bytes 4194320 | tf_op jit(solution)/shard_map/psum | solution.py:141
  466.5 69.1 %all-gather.9.cloned.1.call-done = bf16[1024,2048]{1,0:T(8,128)(2,1)} async-done(((bf16[64,2048]{1,0:T(8,128)(2,1)}), bf16[1024,2048]{1,0:T(8,128)(2,1)}) %all-gather.9.cloned.1.call-update) | async-done | bytes 4194320 | tf_op jit(solution)/shard_map/all_gather | solution.py:108
  535.5 50.9 %multiply_convert_fusion.1 = (bf16[2048,2048]{1,0:T(8,128)(2,1)}, f32[2048,2048]{1,0:T(8,128)}, f32[2048,2048]{1,0:T(8,128)}) fusion(f32[2048]{0:T(1024)S(1)} %copy-done.25, bf16[1024,2048]{1,0:T(8,128)(2,1)} %all-gather.9.cloned.1.call-done, f32[2048,1024]{1,0:T(8,128)} %get-tuple-element.210, f32[1024]{0:T(1024)S(1)} %copy-done.22, ...), kind=kOutput, calls=%fused_computation.36 | convolution fusion | flops 8875147264 | bytes 54550528 | tf_op jit(solution)/shard_map/dot_general | solution.py:146
  586.4 26.5 %all-gather.11.cloned.1.call-done = bf16[2048,1024]{0,1:T(8,128)(2,1)} async-done(((bf16[2048,64]{0,1:T(8,128)(2,1)}), bf16[2048,1024]{0,1:T(8,128)(2,1)}) %all-gather.11.cloned.1.call-update) | async-done | bytes 4194320 | tf_op jit(solution)/shard_map/all_gather | solution.py:109
  612.9 13.9 convolution_convert_fusion.3
  626.8 27.1 %all-reduce.10.cloned.1.call-done = bf16[2048,1024]{1,0:T(8,128)(2,1)} async-done(((bf16[2048,1024]{1,0:T(8,128)(2,1)}), bf16[2048,1024]{1,0:T(8,128)(2,1)}) %all-reduce.10.cloned.1.call-update) | async-done | bytes 4194320 | tf_op jit(solution)/shard_map/psum | solution.py:150
  671.5 25.2 %convert_reduce_fusion = (f32[2048]{0:T(1024)}, bf16[2048,2048]{1,0:T(8,128)(2,1)}) fusion(f32[2048,2048]{1,0:T(8,128)} %get-tuple-element.208, bf16[2048,1024]{0,1:T(8,128)(2,1)} %all-gather.11.cloned.1.call-done, f32[2048,1024]{1,0:T(8,128)S(1)} %get-tuple-element.204, f32[2048]{0:T(1024)S(1)} %negate_multiply_fusion.2, ...), kind=kOutput, calls=%fused_computation.34 | convolution fusion | flops 8665430016 | bytes 54550528 | tf_op jit(solution)/shard_map/dot_general | solution.py:24
  696.7 13.8 convolution_convert_fusion.2
  710.6 29.8 %all-reduce.12.cloned.1.call-done = bf16[2048,1024]{1,0:T(8,128)(2,1)} async-done(((bf16[2048,1024]{1,0:T(8,128)(2,1)}), bf16[2048,1024]{1,0:T(8,128)(2,1)}) %all-reduce.12.cloned.1.call-update) | async-done | bytes 4194320 | tf_op jit(solution)/shard_map/psum | solution.py:171
  740.3 10.1 multiply_reduce_fusion.1
  765.4 53.3 %all_to_all.132 = bf16[16,128,512]{1,0,2:T(8,128)(2,1)S(1)} all-to-all(bf16[16,128,512]{1,0,2:T(8,128)(2,1)S(1)} %copy.63), channel_id=1, replica_groups=mesh['shard'=4,'context'=4,'tensor'=2] {'context'}, dimensions={2} | all-to-all | bytes 4194304 | tf_op jit(solution)/shard_map/all_to_all | solution.py:178
  825.8 150.9 %while.27 = (s32[]{:T(128)}, bf16[16,512,128]{1,2,0:T(8,128)(2,1)S(1)}, bf16[16,512,128]{1,2,0:T(8,128)(2,1)}, bf16[16,512,128]{1,2,0:T(8,128)(2,1)}, bf16[16,51...) while((s32[]{:T(128)}, ...), condition=%wide.region_17.18_spmd, body=%wide.region_15.17_spmd.sunk | while | flops 340590080 | bytes 18896532 | solution.py:181
  988.1 43.3 %all-to-all-done.5 = bf16[16,512,128]{2,0,1:T(8,128)(2,1)S(1)} async-done(((bf16[16,512,128]{2,0,1:T(8,128)(2,1)}), bf16[16,512,128]{2,0,1:T(8,128)(2,1)S(1)}, u32[]{:S(2)}, u32[]{:S(2)}) %all-to-all-start.5) | async-done | bytes 2097184 | tf_op jit(solution)/shard_map/all_to_all | solution.py:185
  1040.4 43.2 %all-to-all-done.7 = bf16[16,512,128]{2,0,1:T(8,128)(2,1)} async-done(((bf16[16,512,128]{2,0,1:T(8,128)(2,1)}), bf16[16,512,128]{2,0,1:T(8,128)(2,1)}, u32[]{:S(2)}, u32[]{:S(2)}) %all-to-all-start.7) | async-done | bytes 2097184 | tf_op jit(solution)/shard_map/all_to_all | solution.py:187
  1096.1 39.7 %all-to-all-done.6 = bf16[16,512,128]{2,0,1:T(8,128)(2,1)} async-done(((bf16[16,512,128]{2,0,1:T(8,128)(2,1)}), bf16[16,512,128]{2,0,1:T(8,128)(2,1)}, u32[]{:S(2)}, u32[]{:S(2)}) %all-to-all-start.6) | async-done | bytes 2097184 | tf_op jit(solution)/shard_map/all_to_all | solution.py:186
  1151.2 8.8 add_convert_fusion.2
  1173.5 9.7 copy.71
  1183.3 8.6 fusion.31
  1192.2 15.9 fusion.53
  1208.8 16.2 fusion.54
  1241.6 78.9 %all-reduce.1 = (f32[2,512]{1,0:T(2,128)}, f32[1024]{0:T(1024)}, f32[2048]{0:T(1024)}, f32[1024]{0:T(1024)}, f32[1024]{0:T(1024)}, /*index=5*/f32[1024]{0:T(1024)}, f32[1024]{0:T(1024)}, f32[1024]{0:T(1024)}) all-reduce(f32[2,512]{1,0:T(2,128)S(1)} %pad_maximum_fusion.1, ...), channel_id=1, replica_groups=mesh['shard'=4,'context'=4,'tensor'=2] {'shard','context'}, use_global_device_ids=true, to_apply=%region_22.23 | all-reduce | flops 9216 | bytes 73728 | tf_op jit(solution)/shard_map/psum | solution.py:212
  1320.5 132.2 %all-reduce.16.cloned.1.call-done = f32[3,1024,512]{2,0,1:T(4,128)} async-done(((f32[3,1024,512]{2,0,1:T(4,128)}), f32[3,1024,512]{2,0,1:T(4,128)}) %all-reduce.16.cloned.1.call-update) | async-done | bytes 6291472
  1454.7 84.0 %reduce-scatter.4.cloned.1.call-done = f32[512,64]{0,1:T(8,128)} async-done(((f32[512,1024]{0,1:T(8,128)}), f32[512,64]{0,1:T(8,128)}) %reduce-scatter.4.cloned.1.call-update) | async-done | bytes 131088 | tf_op jit(solution)/shard_map/reduce_scatter | solution.py:208
  1538.7 181.8 %reduce-scatter.8.cloned.1.call-done = f32[2048,64]{0,1:T(8,128)} async-done(((f32[2048,1024]{0,1:T(8,128)}), f32[2048,64]{0,1:T(8,128)}) %reduce-scatter.8.cloned.1.call-update) | async-done | bytes 524304 | tf_op jit(solution)/shard_map/reduce_scatter | solution.py:210
  1720.4 182.5 %reduce-scatter.6.cloned.1.call-done = f32[64,2048]{1,0:T(8,128)} async-done(((f32[1024,2048]{1,0:T(8,128)}), f32[64,2048]{1,0:T(8,128)}) %reduce-scatter.6.cloned.1.call-update) | async-done | bytes 524304 | tf_op jit(solution)/shard_map/reduce_scatter | solution.py:209
  (534 shorter events, 449.8 us)
Async XLA Ops:
  7.2 74.1 %all-gather.5.cloned.1.call-start = ((), (), s32[]{:S(2)}) async-start(), calls=%async_computation.11 | async-start | bytes 3342336 | tf_op jit(solution)/shard_map/all_gather | solution.py:106
  89.1 51.6 %all-to-all-start.1 = ((bf16[16,128,512]{1,0,2:T(8,128)(2,1)}), bf16[16,128,512]{1,0,2:T(8,128)(2,1)S(1)}, u32[]{:S(2)}, u32[]{:S(2)}) async-start(bf16[16,128,512]{1,0,2:T(8,128)(2,1)} %copy.57), calls=%async_computation.1 | async-start | bytes 4194304 | tf_op jit(solution)/shard_map/all_to_all | solution.py:124
  140.7 52.2 %all-to-all-start = ((bf16[16,128,512]{1,0,2:T(8,128)(2,1)}), bf16[16,128,512]{1,0,2:T(8,128)(2,1)}, u32[]{:S(2)}, u32[]{:S(2)}) async-start(bf16[16,128,512]{1,0,2:T(8,128)(2,1)} %copy.55), calls=%async_computation | async-start | bytes 4194304 | tf_op jit(solution)/shard_map/all_to_all | solution.py:130
  192.9 52.7 %all-to-all-start.2 = ((bf16[16,128,512]{1,0,2:T(8,128)(2,1)}), bf16[16,128,512]{1,0,2:T(8,128)(2,1)}, u32[]{:S(2)}, u32[]{:S(2)}) async-start(bf16[16,128,512]{1,0,2:T(8,128)(2,1)} %copy.59), calls=%async_computation.2 | async-start | bytes 4194304 | tf_op jit(solution)/shard_map/all_to_all | solution.py:127
  208.1 43.1 %copy-start.26 = (s32[16]{0:T(128)S(1)}, s32[16]{0:T(128)}, u32[]{:S(2)}) copy-start(s32[16]{0:T(128)} %param.20) | copy-start | bytes 196
  343.1 53.6 %all-to-all-start.3 = ((bf16[16,512,128]{2,0,1:T(8,128)(2,1)}), bf16[16,512,128]{2,0,1:T(8,128)(2,1)S(1)}, u32[]{:S(2)}, u32[]{:S(2)}) async-start(bf16[16,512,128]{2,0,1:T(8,128)(2,1)} %copy.61), calls=%async_computation.3 | async-start | bytes 4194304 | tf_op jit(solution)/shard_map/all_to_all | solution.py:135
  346.7 75.0 %all-gather.7.cloned.1.call-start = ((), (), s32[]{:S(2)}) async-start(), calls=%async_computation.12 | async-start | bytes 1114112 | tf_op jit(solution)/shard_map/all_gather | solution.py:107
  347.4 108.0 %all-reduce.8.cloned.1.call-start = ((), (), s32[]{:S(2)}) async-start(), calls=%async_computation.13 | async-start | bytes 8388608 | tf_op jit(solution)/shard_map/psum | solution.py:141
  421.7 33.7 %copy-start.18 = (f32[1024]{0:T(1024)S(1)}, f32[1024]{0:T(1024)}, u32[]{:S(2)}) copy-start(f32[1024]{0:T(1024)} %param.24) | copy-start | bytes 12292
  428.0 107.5 %all-gather.9.cloned.1.call-start = ((), (), s32[]{:S(2)}) async-start(), calls=%async_computation.14 | async-start | bytes 4456448 | tf_op jit(solution)/shard_map/all_gather | solution.py:108
  428.6 184.3 %all-gather.11.cloned.1.call-start = ((), (), s32[]{:S(2)}) async-start(), calls=%async_computation.15 | async-start | bytes 4456448 | tf_op jit(solution)/shard_map/all_gather | solution.py:109
  429.2 224.8 %all-reduce.10.cloned.1.call-start = ((), (), s32[]{:S(2)}) async-start(), calls=%async_computation.16 | async-start | bytes 8388608 | tf_op jit(solution)/shard_map/psum | solution.py:150
  461.3 74.2 %copy-start.12 = (f32[1024]{0:T(1024)S(1)}, f32[1024]{0:T(1024)}, u32[]{:S(2)}) copy-start(f32[1024]{0:T(1024)} %param.29) | copy-start | bytes 12292
  461.3 74.2 %copy-start.22 = (f32[1024]{0:T(1024)S(1)}, f32[1024]{0:T(1024)}, u32[]{:S(2)}) copy-start(f32[1024]{0:T(1024)} %param.30) | copy-start | bytes 12292
  461.3 74.2 %copy-start.25 = (f32[2048]{0:T(1024)S(1)}, f32[2048]{0:T(1024)}, u32[]{:S(2)}) copy-start(f32[2048]{0:T(1024)} %param.26) | copy-start | bytes 24580
  612.9 41.1 %copy-start.20 = (f32[1024]{0:T(1024)S(1)}, f32[1024]{0:T(1024)}, u32[]{:S(2)}) copy-start(f32[1024]{0:T(1024)} %param.28) | copy-start | bytes 12292
  626.8 113.5 %all-reduce.12.cloned.1.call-start = ((), (), s32[]{:S(2)}) async-start(), calls=%async_computation.17 | async-start | bytes 8388608 | tf_op jit(solution)/shard_map/psum | solution.py:171
  671.5 25.2 %copy-start = (f32[2048,1024]{1,0:T(8,128)}, f32[2048,1024]{1,0:T(8,128)S(1)}, u32[]{:S(2)}) copy-start(f32[2048,1024]{1,0:T(8,128)S(1)} %get-tuple-element.204) | copy-start | bytes 25165828
  710.6 39.8 %copy-start.11 = (f32[2048]{0:T(1024)S(1)}, f32[2048]{0:T(1024)}, u32[]{:S(2)}) copy-start(f32[2048]{0:T(1024)} %copy-done.10) | copy-start | bytes 24580
  740.3 10.1 copy-start.3
  979.8 51.6 %all-to-all-start.5 = ((bf16[16,512,128]{2,0,1:T(8,128)(2,1)}), bf16[16,512,128]{2,0,1:T(8,128)(2,1)S(1)}, u32[]{:S(2)}, u32[]{:S(2)}) async-start(bf16[16,512,128]{2,0,1:T(8,128)(2,1)} %copy.65), calls=%async_computation.5 | async-start | bytes 4194304 | tf_op jit(solution)/shard_map/all_to_all | solution.py:185
  1031.4 52.2 %all-to-all-start.7 = ((bf16[16,512,128]{2,0,1:T(8,128)(2,1)}), bf16[16,512,128]{2,0,1:T(8,128)(2,1)}, u32[]{:S(2)}, u32[]{:S(2)}) async-start(bf16[16,512,128]{2,0,1:T(8,128)(2,1)} %copy.69), calls=%async_computation.7 | async-start | bytes 4194304 | tf_op jit(solution)/shard_map/all_to_all | solution.py:187
  1083.6 52.2 %all-to-all-start.6 = ((bf16[16,512,128]{2,0,1:T(8,128)(2,1)}), bf16[16,512,128]{2,0,1:T(8,128)(2,1)}, u32[]{:S(2)}, u32[]{:S(2)}) async-start(bf16[16,512,128]{2,0,1:T(8,128)(2,1)} %copy.67), calls=%async_computation.6 | async-start | bytes 4194304 | tf_op jit(solution)/shard_map/all_to_all | solution.py:186
  1088.1 145.7 %all-reduce.14.cloned.1.call-start = ((), (), s32[]{:S(2)}) async-start(), calls=%async_computation.18 | async-start | bytes 8388608 | tf_op jit(solution)/shard_map/psum | solution.py:203
  1160.0 292.7 %all-reduce.16.cloned.1.call-start = ((), (), s32[]{:S(2)}) async-start(), calls=%async_computation.22 | async-start | bytes 16777216
  1183.2 355.4 %reduce-scatter.4.cloned.1.call-start = ((), (), s32[]{:S(2)}) async-start(), calls=%async_computation.19 | async-start | bytes 2228224 | tf_op jit(solution)/shard_map/reduce_scatter | solution.py:208
  1191.9 528.5 %reduce-scatter.8.cloned.1.call-start = ((), (), s32[]{:S(2)}) async-start(), calls=%async_computation.21 | async-start | bytes 8912896 | tf_op jit(solution)/shard_map/reduce_scatter | solution.py:210
  1208.1 694.8 %reduce-scatter.6.cloned.1.call-start = ((), (), s32[]{:S(2)}) async-start(), calls=%async_computation.20 | async-start | bytes 8912896 | tf_op jit(solution)/shard_map/reduce_scatter | solution.py:209
  1233.7 7.8 copy-start.14
  1233.7 7.8 copy-start.15
  1233.8 7.8 copy-start.16
  1233.8 7.8 copy-start.17
  (16 other events, 68.3 us)
Sparse Core Ops, SparseCore 0:
  10.8 70.3 all-gather.4
  350.3 71.3 all-gather.6
  428.1 27.2 all-reduce.7
  458.4 77.0 all-gather.8
  538.5 74.3 all-gather.10
  626.9 27.0 all-reduce.9
  710.7 29.6 all-reduce.11
  1160.1 27.4 all-reduce.13
  1193.6 259.0 all-reduce.15
  1455.4 83.2 reduce-scatter.3
  1541.5 178.8 reduce-scatter.7
  1723.2 179.7 reduce-scatter.5
where the time goes:
time: 1920 us; the launch traced here: 1910 us
  waiting for transfers between devices  1140 us (59%)
  matrix products  260 us (14%)
  local copies, waits for them, and re-layouts  221 us (12%)
  blocking collectives  132 us (7%)
  other arithmetic  109 us (6%)
  starting transfers between devices  30.5 us (2%)
    reduce_scatter x1, waiting for transfers between devices, on_device(): lax.psum_scatter(grad_w_up, ('shard', 'context'), scatter_dimension=0, ti...  183 us
    reduce_scatter x1, waiting for transfers between devices, on_device(): lax.psum_scatter(grad_w_down, ('shard', 'context'), scatter_dimension=1,...  182 us
    unnamed x13, waiting for transfers between devices  135 us
    dynamic_slice x128, local copies, waits for them, and re-layouts, on_device(): lax.map(attend_forward, (head_query, head_key, head_value, lengths))  108 us
    reduce_scatter x1, waiting for transfers between devices, on_device(): lax.psum_scatter(grad_w_out, ('shard', 'context'), scatter_dimension=1, t...  84 us
    psum x1, blocking collectives, on_device(): lax.psum((grad_b_qv, grad_b_out, up_bias_gradient, grad_b_down, grad_gain...  78.9 us
    all_gather x1, waiting for transfers between devices, on_device(): lax.all_gather(w_qkv, ('shard', 'context'), axis=1, tiled=True)  72.6 us
    all_gather x1, waiting for transfers between devices, on_device(): lax.all_gather(w_up, ('shard', 'context'), axis=0, tiled=True)  69.1 us
  transfers between devices with their start and end apart: 19, of which 18 were waited for; matrix products, arithmetic and copies ran while one was open for 10% of the time, Pallas kernels for 0%

commit v1 on v0

v1 whole, which is shorter than its diff:
```python
import functools

import jax
import jax.numpy as jnp
from jax import lax
from jax.experimental import pallas as pl
from jax.experimental.pallas import tpu as pltpu
from jax.sharding import PartitionSpec as P

HEAD_DIM = 64
PAIR = 2 * HEAD_DIM
NEG_FILL = -1000000000.0
EPSILON = 1e-12
SCALE = HEAD_DIM ** (-0.5)
BOTH = ("shard", "context")
F32 = jnp.float32
BF16 = jnp.bfloat16


def dot_nn(a, b):
    return jnp.dot(a, b, preferred_element_type=F32)


def dot_nt(a, b):
    return lax.dot_general(a, b, (((1,), (1,)), ((), ())), preferred_element_type=F32)


def dot_tn(a, b):
    return lax.dot_general(a, b, (((0,), (0,)), ((), ())), preferred_element_type=F32)


def lane_half(rows):
    return lax.broadcasted_iota(jnp.int32, (rows, PAIR), 1) < HEAD_DIM


def masked_scores(query, key_head, usable):
    return jnp.where(usable, dot_nt(key_head, query), NEG_FILL)


def forward_kernel(lengths_ref, q_ref, k_ref, v_ref, out_ref, lse_ref):
    length = lengths_ref[pl.program_id(0)]
    count = q_ref.shape[0] * q_ref.shape[2]
    query = q_ref[...].reshape(count, PAIR) * jnp.asarray(SCALE, BF16)
    keys = k_ref[...].reshape(count, PAIR)
    values = v_ref[...].reshape(count, PAIR)
    first = lane_half(count)
    usable = lax.broadcasted_iota(jnp.int32, (count, count), 0) < length
    results = []
    for head in range(2):
        mine = first if head == 0 else jnp.logical_not(first)
        key_head = jnp.where(mine, keys, jnp.zeros_like(keys))
        scores = masked_scores(query, key_head, usable)
        top = jnp.max(scores, 0, keepdims=True)
        weights = jnp.exp(scores - top)
        denom = jnp.sum(weights, 0, keepdims=True)
        lse_ref[0, 0, head : head + 1, :] = top + jnp.log(denom)
        gathered = dot_tn(values, weights.astype(BF16)) * (1.0 / denom)
        results.append(gathered[head * HEAD_DIM : (head + 1) * HEAD_DIM])
    result = jnp.concatenate(results, 0).T
    out_ref[...] = result.astype(BF16).reshape(out_ref.shape)


def backward_kernel(lengths_ref, q_ref, k_ref, v_ref, g_ref, lse_ref, out_ref):
    length = lengths_ref[pl.program_id(0)]
    pair_index = pl.program_id(1)
    pieces, _, piece_len, _ = q_ref.shape
    count = pieces * piece_len
    scale = jnp.asarray(SCALE, BF16)
    query = q_ref[...].reshape(count, PAIR) * scale
    keys = k_ref[...].reshape(count, PAIR)
    values = v_ref[...].reshape(count, PAIR)
    grads = g_ref[...].reshape(count, PAIR)
    scaled_keys = keys * scale
    first = lane_half(count)
    usable = lax.broadcasted_iota(jnp.int32, (count, count), 0) < length
    dquery, dkey, dvalue = [], [], []
    for head in range(2):
        mine = first if head == 0 else jnp.logical_not(first)
        key_head = jnp.where(mine, keys, jnp.zeros_like(keys))
        value_head = jnp.where(mine, values, jnp.zeros_like(values))
        scores = masked_scores(query, key_head, usable)
        probs = jnp.exp(scores - lse_ref[0, 0, head : head + 1, :])
        dprobs = dot_nt(value_head, grads)
        weighted = probs * dprobs
        total = jnp.sum(weighted, 0, keepdims=True)
        dscores = (weighted - probs * total).astype(BF16)
        dvalue.append(dot_nn(probs.astype(BF16), grads))
        dkey.append(dot_nn(dscores, query))
        dquery.append(dot_tn(scaled_keys, dscores)[head * HEAD_DIM : (head + 1) * HEAD_DIM])
    third = out_ref.shape[3] // 3
    block = (pieces, 1, piece_len, PAIR)
    for slot, value in enumerate(
        (
            jnp.concatenate(dquery, 0).T,
            jnp.where(first, dkey[0], dkey[1]),
            jnp.where(first, dvalue[0], dvalue[1]),
        )
    ):
        start = pl.multiple_of(slot * third + pair_index * PAIR, PAIR)
        out_ref[:, :, :, pl.ds(start, PAIR)] = value.astype(BF16).reshape(block)


def attention_specs(shape):
    pieces, _, piece_len, width = shape
    pairs = width // 3 // PAIR
    block = (pieces, 1, piece_len, PAIR)

    def at(offset):
        return pl.BlockSpec(block, lambda s, h: (0, s, 0, offset * pairs + h))

    lse_spec = pl.BlockSpec((1, 1, 2, pieces * piece_len), lambda s, h: (s, h, 0, 0))
    return pairs, at, lse_spec


def attend(lengths, qkv):
    pieces, seqs, piece_len, width = qkv.shape
    count = pieces * piece_len
    pairs, at, lse_spec = attention_specs(qkv.shape)
    return pl.pallas_call(
        forward_kernel,
        grid=(seqs, pairs),
        in_specs=[pl.BlockSpec(memory_space=pltpu.SMEM), at(0), at(1), at(2)],
        out_specs=[at(0), lse_spec],
        out_shape=[
            jax.ShapeDtypeStruct((pieces, seqs, piece_len, width // 3), BF16),
            jax.ShapeDtypeStruct((seqs, pairs, 2, count), F32),
        ],
        compiler_params=pltpu.CompilerParams(vmem_limit_bytes=40 * 1024 * 1024),
        cost_estimate=pl.CostEstimate(
            flops=8 * seqs * pairs * count * count * PAIR,
            bytes_accessed=8 * seqs * pairs * count * PAIR,
            transcendentals=2 * seqs * pairs * count * count,
        ),
    )(lengths, qkv, qkv, qkv)


def attend_back(lengths, qkv, grads, lse):
    pieces, seqs, piece_len, width = qkv.shape
    count = pieces * piece_len
    pairs, at, lse_spec = attention_specs(qkv.shape)
    return pl.pallas_call(
        backward_kernel,
        grid=(seqs, pairs),
        in_specs=[pl.BlockSpec(memory_space=pltpu.SMEM), at(0), at(1), at(2), at(0), lse_spec],
        out_specs=pl.BlockSpec((pieces, 1, piece_len, width), lambda s, h: (0, s, 0, 0)),
        out_shape=jax.ShapeDtypeStruct(qkv.shape, BF16),
        compiler_params=pltpu.CompilerParams(vmem_limit_bytes=40 * 1024 * 1024),
        cost_estimate=pl.CostEstimate(
            flops=20 * seqs * pairs * count * count * PAIR,
            bytes_accessed=14 * seqs * pairs * count * PAIR,
            transcendentals=2 * seqs * pairs * count * count,
        ),
    )(lengths, qkv, qkv, qkv, grads, lse)


def norm_stats(resid):
    center = resid - jnp.mean(resid, -1, keepdims=True)
    inverse = lax.rsqrt(jnp.mean(center * center, -1, keepdims=True) + EPSILON)
    return center * inverse, inverse


def norm_back(normed, inverse, gain, grad):
    scaled = grad * gain
    mean_one = jnp.mean(scaled, -1, keepdims=True)
    mean_two = jnp.mean(scaled * normed, -1, keepdims=True)
    dresid = (scaled - mean_one - normed * mean_two) * inverse
    return dresid, jnp.sum(grad * normed, 0), jnp.sum(grad, 0)


def partner(value):
    return lax.ppermute(value, "tensor", [(0, 1), (1, 0)])


def butterfly(value, sizes):
    for axis, size in sizes:
        bit = 1
        while bit < size:
            value = value + lax.ppermute(value, axis, [(i, i ^ bit) for i in range(size)])
            bit *= 2
    return value


def gather_rows(part):
    return lax.all_gather(part, BOTH, axis=0, tiled=True)


def gelu_parts(pre_act):
    phi_sum = 0.5 * (1.0 + lax.erf(pre_act * (0.5**0.5)))
    density = jnp.exp(-0.5 * pre_act * pre_act) * 0.3989422804014327
    return (pre_act * phi_sum).astype(BF16), (phi_sum + pre_act * density).astype(BF16)


def reduce_rows(own, other):
    summed = (own + partner(other.astype(BF16)).astype(F32)).astype(BF16)
    return lax.psum_scatter(summed, BOTH, scatter_dimension=0, tiled=True).astype(F32)


def on_device(
    sizes,
    inputs,
    lengths,
    w_qkv,
    b_qv,
    w_out,
    b_out,
    w_up,
    b_up,
    w_down,
    down_bias,
    gain_attn,
    shift_attn,
    gain_ffn,
    shift_ffn,
    grad_output,
):
    seq_count, piece_len, model_width = inputs.shape
    pieces = sizes["context"]
    seqs = seq_count // pieces // 2
    rows = pieces * seqs * piece_len
    core = lax.axis_index("tensor")
    group = lax.axis_index("context")
    split = (pieces, 2, seqs, piece_len, model_width)
    four = (pieces, seqs, piece_len)
    axes = (("context", sizes["context"]), ("shard", sizes["shard"]))

    def to_sequences(array):
        half = lax.dynamic_index_in_dim(array.reshape(split), core, 1, keepdims=False)
        return lax.all_to_all(half, "context", split_axis=0, concat_axis=0, tiled=True).reshape(
            rows, model_width
        )

    def to_positions(array):
        own = lax.all_to_all(
            array.reshape(four + (model_width,)), "context", split_axis=0, concat_axis=0, tiled=True
        )
        other = partner(own)
        low = jnp.where(core == 0, own, other)
        high = jnp.where(core == 0, other, own)
        return jnp.stack([low, high], 1).reshape(inputs.shape)

    slots = lengths.reshape(pieces, 2, seqs)
    own_lengths = lax.dynamic_slice(slots, (group, core, 0), (1, 1, seqs)).reshape(seqs)

    head_cols = w_qkv.shape[2]
    qkv_own = gather_rows(w_qkv.transpose(1, 0, 2).reshape(w_qkv.shape[1], 3 * head_cols))
    flat_in = to_sequences(inputs)
    out_own = gather_rows(w_out.T)
    up_own = gather_rows(w_up)
    down_own = gather_rows(w_down.T)
    qkv_other = partner(qkv_own)
    out_other = partner(out_own)
    up_other = partner(up_own)
    down_other = partner(down_own)
    bias_own = jnp.concatenate([b_qv[0], jnp.zeros_like(b_qv[0]), b_qv[1]])
    small_other = partner(jnp.concatenate([bias_own, b_up]))
    bias_other, b_up_other = small_other[: 3 * head_cols], small_other[3 * head_cols :]

    wide = four + (3 * head_cols,)
    proj_own = (dot_nn(flat_in, qkv_own) + bias_own).astype(BF16).reshape(wide)
    attn_own, lse_own = attend(own_lengths, proj_own)
    proj_other = (dot_nn(flat_in, qkv_other) + bias_other).astype(BF16).reshape(wide)
    attn_other, lse_other = attend(own_lengths, proj_other)
    attn_own = attn_own.reshape(rows, head_cols)
    attn_other = attn_other.reshape(rows, head_cols)
    resid_attn = (
        flat_in.astype(F32) + b_out + (dot_nt(attn_own, out_own) + dot_nt(attn_other, out_other))
    )
    normed_attn, inverse_attn = norm_stats(resid_attn)
    hidden = normed_attn * gain_attn + shift_attn
    hidden_low = hidden.astype(BF16)
    activ_own, slope_own = gelu_parts(dot_nn(hidden_low, up_own) + b_up)
    activ_other, slope_other = gelu_parts(dot_nn(hidden_low, up_other) + b_up_other)
    resid_ffn = (
        hidden + down_bias + (dot_nt(activ_own, down_own) + dot_nt(activ_other, down_other))
    )
    normed_ffn, inverse_ffn = norm_stats(resid_ffn)
    outputs = to_positions((normed_ffn * gain_ffn + shift_ffn).astype(BF16))

    grad_flat = to_sequences(grad_output).astype(F32)
    dresid_ffn, grad_gain_ffn, grad_shift_ffn = norm_back(
        normed_ffn, inverse_ffn, gain_ffn, grad_flat
    )
    grad_b_down = jnp.sum(dresid_ffn, 0)
    dbranch_ffn = dresid_ffn.astype(BF16)
    shard_down = reduce_rows(dot_tn(dbranch_ffn, activ_own), dot_tn(dbranch_ffn, activ_other)).T
    dpre_own = (dot_nn(dbranch_ffn, down_own) * slope_own.astype(F32)).astype(BF16)
    dpre_other = (dot_nn(dbranch_ffn, down_other) * slope_other.astype(F32)).astype(BF16)
    shard_up = reduce_rows(dot_tn(hidden_low, dpre_own), dot_tn(hidden_low, dpre_other))
    dhidden = dresid_ffn + (dot_nt(dpre_own, up_own) + dot_nt(dpre_other, up_other))
    dresid_attn, grad_gain_attn, grad_shift_attn = norm_back(
        normed_attn, inverse_attn, gain_attn, dhidden
    )
    grad_b_out = jnp.sum(dresid_attn, 0)
    dbranch_attn = dresid_attn.astype(BF16)
    shard_out = reduce_rows(dot_tn(dbranch_attn, attn_own), dot_tn(dbranch_attn, attn_other)).T

    common = [
        grad_b_out,
        grad_b_down,
        grad_gain_attn,
        grad_shift_attn,
        grad_gain_ffn,
        grad_shift_ffn,
    ]
    up_bias_own = jnp.sum(dpre_own.astype(F32), 0)
    up_bias_other = jnp.sum(dpre_other.astype(F32), 0)
    early = butterfly(
        jnp.concatenate(common + [up_bias_own])
        + partner(jnp.concatenate(common + [up_bias_other])),
        axes,
    )
    sums = early[: 6 * model_width].reshape(6, model_width)
    up_bias_gradient = early[6 * model_width :]

    narrow = four + (head_cols,)
    dattn_own = dot_nn(dbranch_attn, out_own).astype(BF16).reshape(narrow)
    dattn_other = dot_nn(dbranch_attn, out_other).astype(BF16).reshape(narrow)
    dproj_other = attend_back(own_lengths, proj_other, dattn_other, lse_other).reshape(rows, -1)
    dproj_own = attend_back(own_lengths, proj_own, dattn_own, lse_own).reshape(rows, -1)
    shard_qkv = reduce_rows(dot_tn(flat_in, dproj_own), dot_tn(flat_in, dproj_other))
    shard_qkv = shard_qkv.reshape(-1, 3, head_cols).transpose(1, 0, 2)
    grad_inputs = to_positions(
        (dresid_attn + (dot_nt(dproj_own, qkv_own) + dot_nt(dproj_other, qkv_other))).astype(BF16)
    )
    proj_bias_own = jnp.sum(dproj_own.astype(F32), 0)
    proj_bias_other = jnp.sum(dproj_other.astype(F32), 0)
    late = butterfly(proj_bias_own + partner(proj_bias_other), axes).reshape(3, head_cols)
    grad_b_qv = jnp.stack([late[0], late[2]])
    return (
        outputs,
        grad_inputs,
        shard_qkv,
        grad_b_qv,
        shard_out,
        sums[0],
        shard_up,
        up_bias_gradient,
        shard_down,
        sums[1],
        sums[2],
        sums[3],
        sums[4],
        sums[5],
    )


def solution(mesh):
    placed = (
        P("shard", "context", None),
        P("shard"),
        P(None, BOTH, "tensor"),
        P(None, "tensor"),
        P("tensor", BOTH),
        P(),
        P(BOTH, "tensor"),
        P("tensor"),
        P("tensor", BOTH),
        P(),
        P(),
        P(),
        P(),
        P(),
        P("shard", "context", None),
    )
    return jax.shard_map(
        functools.partial(on_device, dict(mesh.shape)),
        mesh=mesh,
        in_specs=placed,
        out_specs=(
            P("shard", "context", None),
            P("shard", "context", None),
            P(None, BOTH, "tensor"),
            P(None, "tensor"),
            P("tensor", BOTH),
            P(),
            P(BOTH, "tensor"),
            P("tensor"),
            P("tensor", BOTH),
            P(),
            P(),
            P(),
            P(),
            P(),
        ),
        check_vma=False,
    )
```

time: 1920 us -> 950 us (0.49)
  waiting for transfers between devices: 1140 us -> 627 us
  local copies, waits for them, and re-layouts: 221 us -> 31.8 us
  blocking collectives: 132 us -> 0 us
  matrix products: 260 us -> 154 us
  other arithmetic: 109 us -> 23.3 us
  Pallas kernels: 0 us -> 55.9 us
    reduce_scatter x3 -> x4, waiting for transfers between devices: 448 us -> 214 us  [reduce_rows(): lax.psum_scatter(summed, BOTH, scatter_dimension=0, tiled=True).astype(F32)]
    unnamed x13 -> x8, waiting for transfers between devices: 135 us -> 2.01 us
    all_to_all x7 -> x4, waiting for transfers between devices: 285 us -> 156 us  [the longest x2 99.3 us: to_positions(): lax.all_to_all(array.reshape(four + (model_width,)), 'context', split_axi...]
    dynamic_slice x128 -> x1, local copies, waits for them, and re-layouts: 108 us -> 1.88 us  [to_sequences(): lax.dynamic_index_in_dim(array.reshape(split), core, 1, keepdims=False)]
    dot_general x130 -> x24, matrix products: 260 us -> 154 us  [the longest x8 56.6 us: dot_nn(): return jnp.dot(a, b, preferred_element_type=F32)]
    psum x4 -> x0, waiting for transfers between devices: 82.9 us -> none  [the longest x1 29.8 us: on_device(): lax.psum(hidden_part.astype(jnp.bfloat16), 'tensor').astype(jnp.float32)]
    psum x1 -> x0, blocking collectives: 78.9 us -> none  [on_device(): lax.psum((grad_b_qv, grad_b_out, up_bias_gradient, grad_b_down, grad_gain...]
    pallas_call x0 -> x4, Pallas kernels: none -> 55.9 us  [the longest x2 32.5 us: attend_back(): pl.pallas_call(backward_kernel, grid=(seqs, pairs), in_specs=[pl.BlockSpe...]
  transfers between devices with their start and end apart: 19 -> 33, of which waited for: 18 -> 21; matrix products, arithmetic and copies ran while one was open for 10% -> 14% of each run, Pallas kernels for 0% -> 4%
where the time goes in v1:
time: 950 us; the launch traced here: 940 us
  waiting for transfers between devices  627 us (66%)
  matrix products  154 us (16%)
  Pallas kernels  55.9 us (6%)
  starting transfers between devices  32.7 us (3%)
  local copies, waits for them, and re-layouts  31.8 us (3%)
  other arithmetic  23.3 us (2%)
  between operations  15.1 us (2%)
    all_gather x4, waiting for transfers between devices, gather_rows(): return lax.all_gather(part, BOTH, axis=0, tiled=True)  219 us
    reduce_scatter x4, waiting for transfers between devices, reduce_rows(): lax.psum_scatter(summed, BOTH, scatter_dimension=0, tiled=True).astype(F32)  214 us
    all_to_all x2, waiting for transfers between devices, to_positions(): lax.all_to_all(array.reshape(four + (model_width,)), 'context', split_axi...  99.3 us
    all_to_all x2, waiting for transfers between devices, to_sequences(): lax.all_to_all(half, 'context', split_axis=0, concat_axis=0, tiled=True)  57.1 us
    dot_general x8, matrix products, dot_nn(): return jnp.dot(a, b, preferred_element_type=F32)  56.6 us
    dot_general x8, matrix products, dot_nt(): lax.dot_general(a, b, (((1,), (1,)), ((), ())), preferred_element_type=F32)  49.1 us
    dot_general x8, matrix products, dot_tn(): lax.dot_general(a, b, (((0,), (0,)), ((), ())), preferred_element_type=F32)  48.1 us
    pallas_call x2, Pallas kernels, attend_back(): pl.pallas_call(backward_kernel, grid=(seqs, pairs), in_specs=[pl.BlockSpe...  32.5 us
  transfers between devices with their start and end apart: 33, of which 21 were waited for; matrix products, arithmetic and copies ran while one was open for 14% of the time, Pallas kernels for 4%

profile of v1, /device:TPU:0, one launch (start us, length us, event | category | flops | bytes accessed | tf_op | source)
XLA Modules:
  0.0 939.7 jit_solution(6680671985106634925)
XLA Ops:
  14.8 6.3 all-to-all-start
  24.9 57.1 %all-to-all-done = bf16[4,2,128,1024]{2,3,1,0:T(8,128)(2,1)S(1)} async-done(((bf16[4,2,128,1024]{2,3,1,0:T(8,128)(2,1)}), bf16[4,2,128,1024]{2,3,1,0:T(8,128)(2,1)S(1)}, u32[]{:S(2)}, u32[]{:S(2)}) %all-to-all-start) | async-done | bytes 2097184 | tf_op jit(solution)/shard_map/all_to_all | solution.py:228
  87.0 39.1 %all-gather.5.cloned.1.call-done = bf16[1024,1536]{1,0:T(8,128)(2,1)} async-done(((bf16[64,1536]{1,0:T(8,128)(2,1)}), bf16[1024,1536]{1,0:T(8,128)(2,1)}) %all-gather.5.cloned.1.call-update) | async-done | bytes 3145744 | tf_op jit(solution)/shard_map/all_gather | solution.py:184
  131.5 52.5 %all-gather.7.cloned.1.call-done = bf16[1024,512]{1,0:T(8,128)(2,1)} async-done(((bf16[64,512]{1,0:T(8,128)(2,1)}), bf16[1024,512]{1,0:T(8,128)(2,1)}) %all-gather.7.cloned.1.call-update) | async-done | bytes 1048592 | tf_op jit(solution)/shard_map/all_gather | solution.py:184
  189.4 5.9 add_convert_fusion.3
  195.3 11.7 %shard_map.254 = (bf16[4,2,128,512]{3,2,1,0:T(8,128)(2,1)S(1)}, f32[2,4,2,512]{3,2,1,0:T(2,128)S(1)}) custom-call(s32[2]{0:T(128)S(1)} %fusion.19.lengths_ref, bf16[4,2,128,1536]{3,2,1,0:T(8,128)(2,1)S(1)} %bitcast.117, bf16[4,2,128,1536]{3,2,1,0:T(8,128)(2,1)S(1)} %bitcast.118, bf16[4,2,128,1536]{3,2,1,0:T(8,128)(2,1)S(1)} %bitcast.119), custom_call_target="tpu_custom_call" | custom-call | flops 2147483648 | bytes 4194304 | tf_op jit(solution)/shard_map/pallas_call | solution.py:119
  211.3 50.2 %all-gather.11.cloned.1.call-done = bf16[1024,2048]{1,0:T(8,128)(2,1)} async-done(((bf16[64,2048]{1,0:T(8,128)(2,1)}), bf16[1024,2048]{1,0:T(8,128)(2,1)}) %all-gather.11.cloned.1.call-update) | async-done | bytes 4194320 | tf_op jit(solution)/shard_map/all_gather | solution.py:184
  261.5 77.1 %all-gather.9.cloned.1.call-done = bf16[1024,2048]{1,0:T(8,128)(2,1)} async-done(((bf16[64,2048]{1,0:T(8,128)(2,1)}), bf16[1024,2048]{1,0:T(8,128)(2,1)}) %all-gather.9.cloned.1.call-update) | async-done | bytes 4194320 | tf_op jit(solution)/shard_map/all_gather | solution.py:184
  338.7 5.9 add_convert_fusion.2
  344.6 11.7 %shard_map.255 = (bf16[4,2,128,512]{3,2,1,0:T(8,128)(2,1)S(1)}, f32[2,4,2,512]{3,2,1,0:T(2,128)S(1)}) custom-call(s32[2]{0:T(128)S(1)} %fusion.19.lengths_ref, bf16[4,2,128,1536]{3,2,1,0:T(8,128)(2,1)S(1)} %bitcast.123, bf16[4,2,128,1536]{3,2,1,0:T(8,128)(2,1)S(1)} %bitcast.124, bf16[4,2,128,1536]{3,2,1,0:T(8,128)(2,1)S(1)} %bitcast.125), custom_call_target="tpu_custom_call" | custom-call | flops 2147483648 | bytes 4194304 | tf_op jit(solution)/shard_map/pallas_call | solution.py:119
  362.0 7.7 multiply_convert_fusion.3
  369.7 6.1 fusion.29
  375.9 9.0 multiply_convert_fusion.2
  386.9 8.4 fusion.27
  402.3 12.3 %convert_reduce_fusion = (f32[2048]{0:T(1024)S(1)}, bf16[1024,2048]{1,0:T(8,128)(2,1)}) fusion(f32[1024,2048]{1,0:T(8,128)} %get-tuple-element.68, f32[2048]{0:T(1024)S(1)} %slice.74, bf16[1024,1024]{1,0:T(8,128)(2,1)S(1)} %convert_element_type.130, bf16[1024,2048]{1,0:T(8,128)(2,1)} %collective-permute-done.4), kind=kOutput, calls=%fused_computation.14 | convolution fusion | flops 4326422528 | bytes 18890752 | tf_op jit(solution)/shard_map/dot_general | solution.py:21
  414.6 9.4 %convert_reduce_fusion.1 = (f32[2048]{0:T(1024)S(1)}, bf16[1024,2048]{1,0:T(8,128)(2,1)S(1)}) fusion(f32[1024,2048]{1,0:T(8,128)} %get-tuple-element.66, f32[2048]{0:T(1024)S(1)} %copy-done.25, bf16[1024,1024]{1,0:T(8,128)(2,1)S(1)} %convert_element_type.130, bf16[1024,2048]{1,0:T(8,128)(2,1)S(1)} %copy-done.32), kind=kOutput, calls=%fused_computation.15 | convolution fusion | flops 4326422528 | bytes 18890752 | tf_op jit(solution)/shard_map/dot_general | solution.py:21
  424.1 6.1 fusion.30
  430.2 12.4 %multiply_reduce_fusion = (f32[1024]{0:T(1024)S(1)}, f32[1024]{0:T(1024)S(1)}, f32[1024]{0:T(1024)S(1)}, f32[1024]{0:T(1024)S(1)}, f32[1024,1024]{1,0:T(8,128)}) fusion(f32[1024,1024]{1,0:T(8,128)S(1)} %get-tuple-element.64, f32[1024]{0:T(1024)S(1)} %add_rsqrt_fusion.1, f32[1024]{0:T(1024)S(1)} %broadcast_multiply_fusion.5, f32[1024]{0:T(1024)S(1)} %copy-done.22, ...), kind=kOutput, calls=%fused_computation.42 | convolution fusion | flops 4306497536 | bytes 25194496 | tf_op jit(solution)/shard_map/dot_general | solution.py:25
  449.3 16.3 %shard_map.257 = bf16[4,2,128,1536]{3,2,1,0:T(8,128)(2,1)S(1)} custom-call(s32[2]{0:T(128)S(1)} %fusion.19.lengths_ref, bf16[4,2,128,1536]{3,2,1,0:T(8,128)(2,1)S(1)} %bitcast.126, bf16[4,2,128,1536]{3,2,1,0:T(8,128)(2,1)S(1)} %bitcast.127, bf16[4,2,128,1536]{3,2,1,0:T(8,128)(2,1)S(1)} %bitcast.128, bf16[4,2,128,512]{3,2,1,0:T(8,128)(2,1)S(1)} %bitcast.136, ...), custom_call_target="tpu_custom_call" | custom-call | flops 5368709120 | bytes 7340032 | tf_op jit(solution)/shard_map/pallas_call | solution.py:141
  483.3 16.1 %shard_map.256 = bf16[4,2,128,1536]{3,2,1,0:T(8,128)(2,1)S(1)} custom-call(s32[2]{0:T(128)S(1)} %fusion.19.lengths_ref, bf16[4,2,128,1536]{3,2,1,0:T(8,128)(2,1)S(1)} %bitcast.120, bf16[4,2,128,1536]{3,2,1,0:T(8,128)(2,1)S(1)} %bitcast.121, bf16[4,2,128,1536]{3,2,1,0:T(8,128)(2,1)S(1)} %bitcast.122, bf16[4,2,128,512]{3,2,1,0:T(8,128)(2,1)S(1)} %bitcast.135, ...), custom_call_target="tpu_custom_call" | custom-call | flops 5368709120 | bytes 7340032 | tf_op jit(solution)/shard_map/pallas_call | solution.py:141
  501.1 6.4 fusion.10
  507.7 7.6 convolution_convert_fusion
  515.8 6.8 collective-permute-done.20
  522.5 6.4 add_convert_fusion
  530.5 8.6 convolution_convert_fusion.1
  543.0 6.6 add_convert_fusion.4
  554.2 10.7 %add_convert_fusion.1 = bf16[1024,2048]{1,0:T(8,128)(2,1)} fusion(bf16[1024,2048]{1,0:T(8,128)(2,1)} %collective-permute-done.19, bf16[1024,1024]{1,0:T(8,128)(2,1)} %copy-done.16, bf16[1024,2048]{1,0:T(8,128)(2,1)} %copy-done.41), kind=kOutput, calls=%fused_computation.13 | convolution fusion | flops 4301258752 | bytes 14680064 | tf_op jit(solution)/shard_map/dot_general | solution.py:29
  565.0 46.3 %all-to-all-done.3 = bf16[4,2,128,1024]{3,2,1,0:T(8,128)(2,1)} async-done(((bf16[4,2,128,1024]{3,2,1,0:T(8,128)(2,1)}), bf16[4,2,128,1024]{3,2,1,0:T(8,128)(2,1)}, u32[]{:S(2)}, u32[]{:S(2)}) %all-to-all-start.3) | async-done | bytes 2097184 | tf_op jit(solution)/shard_map/all_to_all | solution.py:233
  615.8 53.0 %all-to-all-done.1 = bf16[4,2,128,1024]{3,2,1,0:T(8,128)(2,1)} async-done(((bf16[4,2,128,1024]{3,2,1,0:T(8,128)(2,1)}), bf16[4,2,128,1024]{3,2,1,0:T(8,128)(2,1)}, u32[]{:S(2)}, u32[]{:S(2)}) %all-to-all-start.1) | async-done | bytes 2097184 | tf_op jit(solution)/shard_map/all_to_all | solution.py:233
  713.1 22.8 %reduce-scatter.5.cloned.1.call-done = bf16[64,1536]{1,0:T(8,128)(2,1)} async-done(((bf16[1024,1536]{1,0:T(8,128)(2,1)}), bf16[64,1536]{1,0:T(8,128)(2,1)}) %reduce-scatter.5.cloned.1.call-update) | async-done | bytes 196624 | tf_op jit(solution)/shard_map/reduce_scatter | solution.py:195
  738.0 95.8 %reduce-scatter.11.cloned.1.call-done = bf16[64,2048]{1,0:T(8,128)(2,1)} async-done(((bf16[1024,2048]{1,0:T(8,128)(2,1)}), bf16[64,2048]{1,0:T(8,128)(2,1)}) %reduce-scatter.11.cloned.1.call-update) | async-done | bytes 262160 | tf_op jit(solution)/shard_map/reduce_scatter | solution.py:195
  835.6 95.3 %reduce-scatter.9.cloned.1.call-done = bf16[64,2048]{1,0:T(8,128)(2,1)} async-done(((bf16[1024,2048]{1,0:T(8,128)(2,1)}), bf16[64,2048]{1,0:T(8,128)(2,1)}) %reduce-scatter.9.cloned.1.call-update) | async-done | bytes 262160 | tf_op jit(solution)/shard_map/reduce_scatter | solution.py:195
  (220 shorter events, 136.8 us)
Async XLA Ops:
  7.2 119.0 %all-gather.5.cloned.1.call-start = ((), (), s32[]{:S(2)}) async-start(), calls=%async_computation.8 | async-start | bytes 3342336 | tf_op jit(solution)/shard_map/all_gather | solution.py:184
  8.9 175.1 %all-gather.7.cloned.1.call-start = ((), (), s32[]{:S(2)}) async-start(), calls=%async_computation.9 | async-start | bytes 1114112 | tf_op jit(solution)/shard_map/all_gather | solution.py:184
  9.6 251.9 %all-gather.11.cloned.1.call-start = ((), (), s32[]{:S(2)}) async-start(), calls=%async_computation.11 | async-start | bytes 4456448 | tf_op jit(solution)/shard_map/all_gather | solution.py:184
  14.8 67.2 %all-to-all-start = ((bf16[4,2,128,1024]{2,3,1,0:T(8,128)(2,1)}), bf16[4,2,128,1024]{2,3,1,0:T(8,128)(2,1)S(1)}, u32[]{:S(2)}, u32[]{:S(2)}) async-start(bf16[4,2,128,1024]{2,3,1,0:T(8,128)(2,1)} %bitcast.138), calls=%async_computation | async-start | bytes 4194304 | tf_op jit(solution)/shard_map/all_to_all | solution.py:228
  21.1 317.5 %all-gather.9.cloned.1.call-start = ((), (), s32[]{:S(2)}) async-start(), calls=%async_computation.10 | async-start | bytes 4456448 | tf_op jit(solution)/shard_map/all_gather | solution.py:184
  83.4 104.6 %all-to-all-start.2 = ((bf16[4,2,128,1024]{3,2,1,0:T(8,128)(2,1)}), bf16[4,2,128,1024]{3,2,1,0:T(8,128)(2,1)S(1)}, u32[]{:S(2)}, u32[]{:S(2)}) async-start(bf16[4,2,128,1024]{3,2,1,0:T(8,128)(2,1)} %dynamic-slice_bitcast_fusion), calls=%async_computation.2 | async-start | bytes 4194304 | tf_op jit(solution)/shard_map/all_to_all | solution.py:228
  87.0 615.1 %reduce-scatter.7.cloned.1.call-start = ((), (), s32[]{:S(2)}) async-start(), calls=%async_computation.13 | async-start | bytes 1114112 | tf_op jit(solution)/shard_map/reduce_scatter | solution.py:195
  126.2 212.5 %collective-permute-start = (bf16[1024,1536]{1,0:T(8,128)(2,1)}, bf16[1024,1536]{1,0:T(8,128)(2,1)}, u32[]{:S(2)}, u32[]{:S(2)}) collective-permute-start(bf16[1024,1536]{1,0:T(8,128)(2,1)} %all-gather.5.cloned.1.call-done), channel_id=1, source_target_pairs={{0,1},{1,0},{2,3},{3,2},{4,5},{5,4},{6,7},{7,6},{8,9},{9,8},{10,11... | collective-permute-start | bytes 9437192 | tf_op jit(solution)/shard_map/ppermute | solution.py:171
  126.2 5.3 collective-permute-start.1
  184.0 172.4 %collective-permute-start.2 = (bf16[1024,512]{1,0:T(8,128)(2,1)}, bf16[1024,512]{1,0:T(8,128)(2,1)}, u32[]{:S(2)}, u32[]{:S(2)}) collective-permute-start(bf16[1024,512]{1,0:T(8,128)(2,1)} %all-gather.7.cloned.1.call-done), channel_id=1, source_target_pairs={{0,1},{1,0},{2,3},{3,2},{4,5},{5,4},{6,7},{7,6},{8,9},{9,8},{10,11... | collective-permute-start | bytes 3145736 | tf_op jit(solution)/shard_map/ppermute | solution.py:171
  261.5 123.3 %collective-permute-start.4 = (bf16[1024,2048]{1,0:T(8,128)(2,1)}, bf16[1024,2048]{1,0:T(8,128)(2,1)}, u32[]{:S(2)}, u32[]{:S(2)}) collective-permute-start(bf16[1024,2048]{1,0:T(8,128)(2,1)} %all-gather.11.cloned.1.call-done), channel_id=1, source_target_pairs={{0,1},{1,0},{2,3},{3,2},{4,5},{5,4},{6,7},{7,6},{8,9},{9,8},{10,11... | collective-permute-start | bytes 12582920 | tf_op jit(solution)/shard_map/ppermute | solution.py:171
  338.7 37.2 %collective-permute-start.3 = (bf16[1024,2048]{1,0:T(8,128)(2,1)}, bf16[1024,2048]{1,0:T(8,128)(2,1)}, u32[]{:S(2)}, u32[]{:S(2)}) collective-permute-start(bf16[1024,2048]{1,0:T(8,128)(2,1)} %all-gather.9.cloned.1.call-done), channel_id=1, source_target_pairs={{0,1},{1,0},{2,3},{3,2},{4,5},{5,4},{6,7},{7,6},{8,9},{9,8},{10,11... | collective-permute-start | bytes 12582920 | tf_op jit(solution)/shard_map/ppermute | solution.py:171
  470.5 28.9 %collective-permute-start.7 = (bf16[1024,1536]{1,0:T(8,128)(2,1)}, bf16[1024,1536]{1,0:T(8,128)(2,1)}, u32[]{:S(2)}, u32[]{:S(2)}) collective-permute-start(bf16[1024,1536]{1,0:T(8,128)(2,1)} %bitcast_convert_fusion), channel_id=1, source_target_pairs={{0,1},{1,0},{2,3},{3,2},{4,5},{5,4},{6,7},{7,6},{8,9},{9,8},{10,11... | collective-permute-start | bytes 9437192 | tf_op jit(solution)/shard_map/ppermute | solution.py:171
  472.3 5.5 collective-permute-start.13
  480.1 255.7 %reduce-scatter.5.cloned.1.call-start = ((), (), s32[]{:S(2)}) async-start(), calls=%async_computation.12 | async-start | bytes 3342336 | tf_op jit(solution)/shard_map/reduce_scatter | solution.py:195
  507.6 326.2 %reduce-scatter.11.cloned.1.call-start = ((), (), s32[]{:S(2)}) async-start(), calls=%async_computation.15 | async-start | bytes 4456448 | tf_op jit(solution)/shard_map/reduce_scatter | solution.py:195
  515.3 7.3 collective-permute-start.20
  539.1 15.1 %collective-permute-start.19 = (bf16[1024,2048]{1,0:T(8,128)(2,1)}, bf16[1024,2048]{1,0:T(8,128)(2,1)}, u32[]{:S(2)}, u32[]{:S(2)}) collective-permute-start(bf16[1024,2048]{1,0:T(8,128)(2,1)} %convolution_convert_fusion.1), channel_id=1, source_target_pairs={{0,1},{1,0},{2,3},{3,2},{4,5},{5,4},{6,7},{7,6},{8,9},{9,8},{10,11... | collective-permute-start | bytes 12582920 | tf_op jit(solution)/shard_map/ppermute | solution.py:171
  549.5 61.7 %all-to-all-start.3 = ((bf16[4,2,128,1024]{3,2,1,0:T(8,128)(2,1)}), bf16[4,2,128,1024]{3,2,1,0:T(8,128)(2,1)}, u32[]{:S(2)}, u32[]{:S(2)}) async-start(bf16[4,2,128,1024]{3,2,1,0:T(8,128)(2,1)} %bitcast.145), calls=%async_computation.3 | async-start | bytes 4194304 | tf_op jit(solution)/shard_map/all_to_all | solution.py:233
  554.0 376.9 %reduce-scatter.9.cloned.1.call-start = ((), (), s32[]{:S(2)}) async-start(), calls=%async_computation.14 | async-start | bytes 4456448 | tf_op jit(solution)/shard_map/reduce_scatter | solution.py:195
  611.3 57.6 %all-to-all-start.1 = ((bf16[4,2,128,1024]{3,2,1,0:T(8,128)(2,1)}), bf16[4,2,128,1024]{3,2,1,0:T(8,128)(2,1)}, u32[]{:S(2)}, u32[]{:S(2)}) async-start(bf16[4,2,128,1024]{3,2,1,0:T(8,128)(2,1)} %bitcast.137), calls=%async_computation.1 | async-start | bytes 4194304 | tf_op jit(solution)/shard_map/all_to_all | solution.py:233
  615.8 87.9 %collective-permute-start.6 = (bf16[4,2,128,1024]{3,2,1,0:T(8,128)(2,1)}, bf16[4,2,128,1024]{3,2,1,0:T(8,128)(2,1)}, u32[]{:S(2)}, u32[]{:S(2)}) collective-permute-start(bf16[4,2,128,1024]{3,2,1,0:T(8,128)(2,1)} %all-to-all-done.3), channel_id=1, source_target_pairs={{0,1},{1,0},{2,3},{3,2},{4,5},{5,4},{6,7},{7,6},{8,9},{9,8},{10,11... | collective-permute-start | bytes 6291464 | tf_op jit(solution)/shard_map/ppermute | solution.py:171
  668.9 34.8 %collective-permute-start.5 = (bf16[4,2,128,1024]{3,2,1,0:T(8,128)(2,1)}, bf16[4,2,128,1024]{3,2,1,0:T(8,128)(2,1)}, u32[]{:S(2)}, u32[]{:S(2)}) collective-permute-start(bf16[4,2,128,1024]{3,2,1,0:T(8,128)(2,1)} %all-to-all-done.1), channel_id=1, source_target_pairs={{0,1},{1,0},{2,3},{3,2},{4,5},{5,4},{6,7},{7,6},{8,9},{9,8},{10,11... | collective-permute-start | bytes 6291464 | tf_op jit(solution)/shard_map/ppermute | solution.py:171
  668.9 3.8 collective-permute-start.14
  672.7 3.9 collective-permute-start.15
  673.2 4.2 collective-permute-start.8
  676.6 16.3 %collective-permute-start.16 = (f32[8192]{0:T(1024)S(1)}, f32[8192]{0:T(1024)S(1)}, u32[]{:S(2)}, u32[]{:S(2)}) collective-permute-start(f32[8192]{0:T(1024)S(1)} %add.215), channel_id=1, source_target_pairs={{0,4},{2,6},{4,0},{6,2},{1,5},{3,7},{5,1},{7,3},{8,12},{10,14},{12... | collective-permute-start | bytes 98312 | tf_op jit(solution)/shard_map/ppermute | solution.py:178
  677.4 3.7 collective-permute-start.9
  681.1 4.5 collective-permute-start.10
  689.3 3.7 collective-permute-start.12
  693.0 4.0 collective-permute-start.17
  697.0 3.9 collective-permute-start.18
  (44 other events, 1060.9 us)
Sparse Core Ops, SparseCore 0:
  11.4 114.6 all-gather.4
  128.9 55.0 all-gather.6
  186.7 74.7 all-gather.10
  264.1 74.4 all-gather.8
  480.2 77.4 reduce-scatter.6
  563.4 172.4 reduce-scatter.4
  738.2 95.5 reduce-scatter.10
  836.2 94.6 reduce-scatter.8

commit v2 on v1

--- a/solution.py
+++ b/solution.py
@@ -180,6 +180,40 @@
     return value
 
 
+def device_bits(sizes):
+    for axis in ("context", "shard"):
+        bit = 1
+        while bit < sizes[axis]:
+            swaps = [(i, i ^ bit) for i in range(sizes[axis])]
+            yield axis, swaps, (lax.axis_index(axis) // bit) % 2
+            bit *= 2
+
+
+def gather_doubling(part, sizes):
+    for axis, swaps, upper in device_bits(sizes):
+        other = lax.ppermute(part, axis, swaps)
+        low = jnp.where(upper == 0, part, other)
+        high = jnp.where(upper == 0, other, part)
+        part = jnp.concatenate([low, high], 0)
+    return part
+
+
+def reduce_halving(own, other, sizes):
+    total = own + partner(other.astype(BF16)).astype(F32)
+    stages = [total]
+    for axis, swaps, upper in reversed(list(device_bits(sizes))):
+        halves = total.reshape((2, total.shape[0] // 2) + total.shape[1:])
+        kept = lax.dynamic_index_in_dim(halves, upper, 0, keepdims=False)
+        sent = lax.dynamic_index_in_dim(halves, 1 - upper, 0, keepdims=False)
+        total = kept + lax.ppermute(sent.astype(BF16), axis, swaps).astype(F32)
+        stages.append(total)
+    return stages
+
+
+def after(value, *earlier):
+    return lax.optimization_barrier((value,) + earlier)[0]
+
+
 def gather_rows(part):
     return lax.all_gather(part, BOTH, axis=0, tiled=True)
 
@@ -190,8 +224,11 @@
     return (pre_act * phi_sum).astype(BF16), (phi_sum + pre_act * density).astype(BF16)
 
 
-def reduce_rows(own, other):
-    summed = (own + partner(other.astype(BF16)).astype(F32)).astype(BF16)
+def pair_sum(own, other):
+    return (own + partner(other.astype(BF16)).astype(F32)).astype(BF16)
+
+
+def scatter_rows(summed):
     return lax.psum_scatter(summed, BOTH, scatter_dimension=0, tiled=True).astype(F32)
 
 
@@ -244,13 +281,11 @@
     head_cols = w_qkv.shape[2]
     qkv_own = gather_rows(w_qkv.transpose(1, 0, 2).reshape(w_qkv.shape[1], 3 * head_cols))
     flat_in = to_sequences(inputs)
-    out_own = gather_rows(w_out.T)
+    out_own = gather_doubling(w_out.T, sizes)
     up_own = gather_rows(w_up)
-    down_own = gather_rows(w_down.T)
+    down_own = gather_doubling(w_down.T, sizes)
     qkv_other = partner(qkv_own)
     out_other = partner(out_own)
-    up_other = partner(up_own)
-    down_other = partner(down_own)
     bias_own = jnp.concatenate([b_qv[0], jnp.zeros_like(b_qv[0]), b_qv[1]])
     small_other = partner(jnp.concatenate([bias_own, b_up]))
     bias_other, b_up_other = small_other[: 3 * head_cols], small_other[3 * head_cols :]
@@ -260,6 +295,10 @@
     attn_own, lse_own = attend(own_lengths, proj_own)
     proj_other = (dot_nn(flat_in, qkv_other) + bias_other).astype(BF16).reshape(wide)
     attn_other, lse_other = attend(own_lengths, proj_other)
+    up_own = after(up_own, attn_other)
+    up_other = partner(up_own)
+    down_own = after(down_own, attn_other)
+    down_other = partner(down_own)
     attn_own = attn_own.reshape(rows, head_cols)
     attn_other = attn_other.reshape(rows, head_cols)
     resid_attn = (
@@ -276,23 +315,30 @@
     normed_ffn, inverse_ffn = norm_stats(resid_ffn)
     outputs = to_positions((normed_ffn * gain_ffn + shift_ffn).astype(BF16))
 
-    grad_flat = to_sequences(grad_output).astype(F32)
+    grad_flat = to_sequences(after(grad_output, proj_own)).astype(F32)
     dresid_ffn, grad_gain_ffn, grad_shift_ffn = norm_back(
         normed_ffn, inverse_ffn, gain_ffn, grad_flat
     )
     grad_b_down = jnp.sum(dresid_ffn, 0)
     dbranch_ffn = dresid_ffn.astype(BF16)
-    shard_down = reduce_rows(dot_tn(dbranch_ffn, activ_own), dot_tn(dbranch_ffn, activ_other)).T
+    down_stages = reduce_halving(
+        dot_tn(dbranch_ffn, activ_own), dot_tn(dbranch_ffn, activ_other), sizes
+    )
+    shard_down = down_stages[-1].T
     dpre_own = (dot_nn(dbranch_ffn, down_own) * slope_own.astype(F32)).astype(BF16)
     dpre_other = (dot_nn(dbranch_ffn, down_other) * slope_other.astype(F32)).astype(BF16)
-    shard_up = reduce_rows(dot_tn(hidden_low, dpre_own), dot_tn(hidden_low, dpre_other))
+    summed_up = pair_sum(dot_tn(hidden_low, dpre_own), dot_tn(hidden_low, dpre_other))
+    shard_up = scatter_rows(summed_up)
     dhidden = dresid_ffn + (dot_nt(dpre_own, up_own) + dot_nt(dpre_other, up_other))
     dresid_attn, grad_gain_attn, grad_shift_attn = norm_back(
         normed_attn, inverse_attn, gain_attn, dhidden
     )
     grad_b_out = jnp.sum(dresid_attn, 0)
     dbranch_attn = dresid_attn.astype(BF16)
-    shard_out = reduce_rows(dot_tn(dbranch_attn, attn_own), dot_tn(dbranch_attn, attn_other)).T
+    out_stages = reduce_halving(
+        dot_tn(dbranch_attn, attn_own), dot_tn(dbranch_attn, attn_other), sizes
+    )
+    shard_out = out_stages[-1].T
 
     common = [
         grad_b_out,
@@ -315,9 +361,13 @@
     narrow = four + (head_cols,)
     dattn_own = dot_nn(dbranch_attn, out_own).astype(BF16).reshape(narrow)
     dattn_other = dot_nn(dbranch_attn, out_other).astype(BF16).reshape(narrow)
+    dattn_other = after(dattn_other, summed_up)
+    dattn_own = after(dattn_own, down_stages[0])
     dproj_other = attend_back(own_lengths, proj_other, dattn_other, lse_other).reshape(rows, -1)
     dproj_own = attend_back(own_lengths, proj_own, dattn_own, lse_own).reshape(rows, -1)
-    shard_qkv = reduce_rows(dot_tn(flat_in, dproj_own), dot_tn(flat_in, dproj_other))
+    dproj_own = after(dproj_own, outputs, down_stages[2])
+    summed_qkv = pair_sum(dot_tn(flat_in, dproj_own), dot_tn(flat_in, dproj_other))
+    shard_qkv = scatter_rows(after(summed_qkv, shard_up))
     shard_qkv = shard_qkv.reshape(-1, 3, head_cols).transpose(1, 0, 2)
     grad_inputs = to_positions(
         (dresid_attn + (dot_nt(dproj_own, qkv_own) + dot_nt(dproj_other, qkv_other))).astype(BF16)

time: 950 us -> 723 us (0.76)
  waiting for transfers between devices: 627 us -> 345 us
  other arithmetic: 23.3 us -> 60.3 us
  starting transfers between devices: 32.7 us -> 56.3 us
    ppermute x0 -> x16, waiting for transfers between devices: none -> 252 us  [the longest x8 171 us: gather_doubling(): other = lax.ppermute(part, axis, swaps)]
    all_gather x4 -> x2, waiting for transfers between devices: 219 us -> 0.01 us  [gather_rows(): return lax.all_gather(part, BOTH, axis=0, tiled=True)]
    reduce_scatter x4 -> x2, waiting for transfers between devices: 214 us -> 14.3 us  [scatter_rows(): lax.psum_scatter(summed, BOTH, scatter_dimension=0, tiled=True).astype(F32)]
    all_to_all x2, waiting for transfers between devices: 99.3 us -> 0.01 us  [to_positions(): lax.all_to_all(array.reshape(four + (model_width,)), 'context', split_axi...]
    ppermute x8, waiting for transfers between devices: 15.7 us -> 69.3 us  [butterfly(): lax.ppermute(value, axis, [(i, i ^ bit) for i in range(size)])]
    all_to_all x2, waiting for transfers between devices: 57.1 us -> 4.79 us  [to_sequences(): lax.all_to_all(half, 'context', split_axis=0, concat_axis=0, tiled=True)]
    ppermute x0 -> x16, starting transfers between devices: none -> 23.1 us  [the longest x8 12.4 us: gather_doubling(): other = lax.ppermute(part, axis, swaps)]
    ppermute x13, waiting for transfers between devices: 20 us -> 5.11 us  [partner(): return lax.ppermute(value, 'tensor', [(0, 1), (1, 0)])]
  transfers between devices with their start and end apart: 33 -> 45, of which waited for: 21 -> 24; matrix products, arithmetic and copies ran while one was open for 14% -> 30% of each run, Pallas kernels for 4% -> 8%
where the time goes in v2:
time: 723 us; the launch traced here: 717 us
  waiting for transfers between devices  345 us (48%)
  matrix products  154 us (21%)
  other arithmetic  60.3 us (8%)
  starting transfers between devices  56.3 us (8%)
  Pallas kernels  55.6 us (8%)
  local copies, waits for them, and re-layouts  29.5 us (4%)
  between operations  15.5 us (2%)
    ppermute x8, waiting for transfers between devices, gather_doubling(): other = lax.ppermute(part, axis, swaps)  171 us
    ppermute x8, waiting for transfers between devices, reduce_halving(): total = kept + lax.ppermute(sent.astype(BF16), axis, swaps).astype(F32)  80.4 us
    ppermute x8, waiting for transfers between devices, butterfly(): lax.ppermute(value, axis, [(i, i ^ bit) for i in range(size)])  69.3 us
    dot_general x8, matrix products, dot_nt(): lax.dot_general(a, b, (((1,), (1,)), ((), ())), preferred_element_type=F32)  55.9 us
    dot_general x8, matrix products, dot_nn(): return jnp.dot(a, b, preferred_element_type=F32)  52.4 us
    dot_general x8, matrix products, dot_tn(): lax.dot_general(a, b, (((0,), (0,)), ((), ())), preferred_element_type=F32)  45.8 us
    pallas_call x2, Pallas kernels, attend_back(): pl.pallas_call(backward_kernel, grid=(seqs, pairs), in_specs=[pl.BlockSpe...  32.2 us
    pallas_call x2, Pallas kernels, attend(): pl.pallas_call(forward_kernel, grid=(seqs, pairs), in_specs=[pl.BlockSpec...  23.4 us
  transfers between devices with their start and end apart: 45, of which 24 were waited for; matrix products, arithmetic and copies ran while one was open for 30% of the time, Pallas kernels for 8%

profile of v2, /device:TPU:0, one launch (start us, length us, event | category | flops | bytes accessed | tf_op | source)
XLA Modules:
  0.0 716.6 jit_solution(17162521382109867374)
XLA Ops:
  12.0 6.5 collective-permute-done.7
  32.7 6.4 collective-permute-done
  39.2 23.7 %collective-permute-done.8 = bf16[128,2048]{1,0:T(8,128)(2,1)} collective-permute-done((bf16[128,2048]{1,0:T(8,128)(2,1)S(1)}, bf16[128,2048]{1,0:T(8,128)(2,1)}, u32[]{:S(2)}, u32[]{:S(2)}) %collective-permute-start.8) | collective-permute-done | bytes 524320 | tf_op jit(solution)/shard_map/ppermute | solution.py:194
  66.8 58.8 %collective-permute-done.1 = bf16[128,512]{1,0:T(8,128)(2,1)S(1)} collective-permute-done((bf16[128,512]{1,0:T(8,128)(2,1)S(1)}, bf16[128,512]{1,0:T(8,128)(2,1)S(1)}, u32[]{:S(2)}, u32[]{:S(2)}) %collective-permute-start.1) | collective-permute-done | bytes 131104 | tf_op jit(solution)/shard_map/ppermute | solution.py:194
  127.8 6.4 collective-permute-done.2
  147.0 69.5 %collective-permute-done.3 = bf16[512,512]{1,0:T(8,128)(2,1)S(1)} collective-permute-done((bf16[512,512]{1,0:T(8,128)(2,1)}, bf16[512,512]{1,0:T(8,128)(2,1)S(1)}, u32[]{:S(2)}, u32[]{:S(2)}) %collective-permute-start.3) | collective-permute-done | bytes 524320 | tf_op jit(solution)/shard_map/ppermute | solution.py:194
  228.5 6.2 all-to-all-start.2
  240.9 11.7 %shard_map.254 = (bf16[4,2,128,512]{3,2,1,0:T(8,128)(2,1)S(1)}, f32[2,4,2,512]{3,2,1,0:T(2,128)S(1)}) custom-call(s32[2]{0:T(128)S(1)} %fusion.28.lengths_ref, bf16[4,2,128,1536]{3,2,1,0:T(8,128)(2,1)S(1)} %bitcast.157, bf16[4,2,128,1536]{3,2,1,0:T(8,128)(2,1)S(1)} %bitcast.158, bf16[4,2,128,1536]{3,2,1,0:T(8,128)(2,1)S(1)} %bitcast.159), custom_call_target="tpu_custom_call" | custom-call | flops 2147483648 | bytes 4194304 | tf_op jit(solution)/shard_map/pallas_call | solution.py:119
  259.1 11.7 %shard_map.255 = (bf16[4,2,128,512]{3,2,1,0:T(8,128)(2,1)S(1)}, f32[2,4,2,512]{3,2,1,0:T(2,128)S(1)}) custom-call(s32[2]{0:T(128)S(1)} %fusion.28.lengths_ref, bf16[4,2,128,1536]{3,2,1,0:T(8,128)(2,1)S(1)} %bitcast.163, bf16[4,2,128,1536]{3,2,1,0:T(8,128)(2,1)S(1)} %bitcast.164, bf16[4,2,128,1536]{3,2,1,0:T(8,128)(2,1)S(1)} %bitcast.165), custom_call_target="tpu_custom_call" | custom-call | flops 2147483648 | bytes 4194304 | tf_op jit(solution)/shard_map/pallas_call | solution.py:119
  291.8 7.4 %multiply_convert_fusion.3 = (bf16[1024,2048]{1,0:T(8,128)(2,1)S(1)}, f32[1024,2048]{1,0:T(8,128)}) fusion(f32[2048]{0:T(1024)S(1)} %copy-done.50, bf16[1024,1024]{1,0:T(8,128)(2,1)S(1)} %fusion.17, bf16[1024,2048]{1,0:T(8,128)(2,1)S(1)} %copy-done.56), kind=kOutput, calls=%fused_computation.20 | convolution fusion | flops 4307550208 | bytes 18882560 | tf_op jit(solution)/shard_map/dot_general | solution.py:21
  303.8 9.0 %multiply_convert_fusion.2 = (bf16[1024,2048]{1,0:T(8,128)(2,1)S(1)}, f32[1024,2048]{1,0:T(8,128)}) fusion(f32[2048]{0:T(1024)S(1)} %slice.74, bf16[1024,1024]{1,0:T(8,128)(2,1)S(1)} %fusion.17, bf16[1024,2048]{1,0:T(8,128)(2,1)} %collective-permute-done.11), kind=kOutput, calls=%fused_computation.18 | convolution fusion | flops 4307550208 | bytes 18882560 | tf_op jit(solution)/shard_map/dot_general | solution.py:21
  312.9 8.8 %fusion.36 = (f32[1024]{0:T(1024)S(1)}, f32[1024,1024]{1,0:T(8,128)S(1)}) fusion(f32[1024,1024]{1,0:T(8,128)S(1)} %fusion.38, bf16[1024,2048]{1,0:T(8,128)(2,1)S(1)} %get-tuple-element.97, bf16[1024,2048]{1,0:T(8,128)(2,1)} %collective-permute-done.12, f32[1024]{0:T(1024)S(1)} %copy-done.59, f32[1024]{0:T(1024)S(1)} %copy-done.53, ...), kind=kOutput, calls=%fused_computation.151 | convolution fusion | flops 4303354880 | bytes 20996096 | tf_op jit(solution)/shard_map/dot_general | solution.py:25
  340.0 6.6 convolution_convert_fusion.1
  346.6 10.2 %convert_reduce_fusion = (f32[2048]{0:T(1024)S(1)}, bf16[1024,2048]{1,0:T(8,128)(2,1)S(1)}) fusion(f32[1024,2048]{1,0:T(8,128)} %get-tuple-element.98, f32[2048]{0:T(1024)S(1)} %slice.74, bf16[1024,1024]{1,0:T(8,128)(2,1)S(1)} %convert_element_type.193, bf16[1024,2048]{1,0:T(8,128)(2,1)} %collective-permute-done.12), kind=kOutput, calls=%fused_computation.12 | convolution fusion | flops 4326422528 | bytes 18890752 | tf_op jit(solution)/shard_map/dot_general | solution.py:21
  356.8 6.3 convolution_convert_fusion
  363.6 8.5 %convert_reduce_fusion.1 = (f32[2048]{0:T(1024)S(1)}, bf16[1024,2048]{1,0:T(8,128)(2,1)}) fusion(f32[1024,2048]{1,0:T(8,128)S(1)} %bitcast.219, f32[2048]{0:T(1024)S(1)} %copy-done.50, bf16[1024,1024]{1,0:T(8,128)(2,1)S(1)} %convert_element_type.193, bf16[1024,2048]{1,0:T(8,128)(2,1)S(1)} %copy-done.32), kind=kOutput, calls=%fused_computation.13 | convolution fusion | flops 4326422528 | bytes 18890752 | tf_op jit(solution)/shard_map/dot_general | solution.py:21
  372.2 8.6 %fusion.39 = f32[1024,1024]{1,0:T(8,128)} fusion(bf16[1024,2048]{1,0:T(8,128)(2,1)} %get-tuple-element.103, bf16[1024,2048]{1,0:T(8,128)(2,1)S(1)} %copy-done.57), kind=kOutput, calls=%fused_computation.154 | convolution fusion | flops 4294967296 | bytes 12582912 | tf_op jit(solution)/shard_map/dot_general | solution.py:25
  380.8 12.5 %multiply_reduce_fusion = (f32[1024]{0:T(1024)S(1)}, f32[1024]{0:T(1024)S(1)}, f32[1024]{0:T(1024)S(1)}, f32[1024]{0:T(1024)S(1)}, f32[1024,1024]{1,0:T(8,128)}) fusion(f32[1024,1024]{1,0:T(8,128)S(1)} %copy-done.14, f32[1024]{0:T(1024)S(1)} %add_rsqrt_fusion.1, f32[1024]{0:T(1024)S(1)} %broadcast_multiply_fusion.5, f32[1024]{0:T(1024)S(1)} %copy-done.46, ...), kind=kOutput, calls=%fused_computation.43 | convolution fusion | flops 4306497536 | bytes 25194496 | tf_op jit(solution)/shard_map/dot_general | solution.py:25
  393.3 7.9 %add_convert_fusion = bf16[1024,2048]{1,0:T(8,128)(2,1)} fusion(bf16[1024,2048]{1,0:T(8,128)(2,1)} %collective-permute-done.17, bf16[1024,1024]{1,0:T(8,128)(2,1)S(1)} %copy-done.39, bf16[1024,2048]{1,0:T(8,128)(2,1)S(1)} %copy-done.63), kind=kOutput, calls=%fused_computation.14 | convolution fusion | flops 4301258752 | bytes 14680064 | tf_op jit(solution)/shard_map/dot_general | solution.py:29
  416.3 8.7 %convert_add_fusion = f32[1024,2048]{1,0:T(8,128)S(1)} fusion(bf16[1024,2048]{1,0:T(8,128)(2,1)} %collective-permute-done.14, bf16[1024,1024]{1,0:T(8,128)(2,1)} %copy-done.19, bf16[1024,2048]{1,0:T(8,128)(2,1)} %copy-done.33), kind=kOutput, calls=%fused_computation.15 | convolution fusion | flops 4299161600 | bytes 18874368 | tf_op jit(solution)/shard_map/dot_general | solution.py:29
  427.2 16.1 %shard_map.257 = bf16[4,2,128,1536]{3,2,1,0:T(8,128)(2,1)S(1)} custom-call(s32[2]{0:T(128)S(1)} %fusion.28.lengths_ref, bf16[4,2,128,1536]{3,2,1,0:T(8,128)(2,1)S(1)} %bitcast.166, bf16[4,2,128,1536]{3,2,1,0:T(8,128)(2,1)S(1)} %bitcast.167, bf16[4,2,128,1536]{3,2,1,0:T(8,128)(2,1)S(1)} %bitcast.168, bf16[4,2,128,512]{3,2,1,0:T(8,128)(2,1)S(1)} %bitcast.178, ...), custom_call_target="tpu_custom_call" | custom-call | flops 5368709120 | bytes 7340032 | tf_op jit(solution)/shard_map/pallas_call | solution.py:141
  448.3 7.2 %fusion.40 = f32[1024,1024]{1,0:T(8,128)} fusion(bf16[1024,1536]{1,0:T(8,128)(2,1)S(1)} %bitcast.169, bf16[1024,1536]{1,0:T(8,128)(2,1)} %collective-permute-done.4), kind=kOutput, calls=%fused_computation.155 | convolution fusion | flops 3221225472 | bytes 10485760 | tf_op jit(solution)/shard_map/dot_general | solution.py:25
  455.5 52.7 %collective-permute-done.15 = bf16[512,2048]{1,0:T(8,128)(2,1)} collective-permute-done((bf16[512,2048]{1,0:T(8,128)(2,1)S(1)}, bf16[512,2048]{1,0:T(8,128)(2,1)}, u32[]{:S(2)}, u32[]{:S(2)}) %collective-permute-start.15) | collective-permute-done | bytes 2097184 | tf_op jit(solution)/shard_map/ppermute | solution.py:208
  510.9 16.1 %shard_map.256 = bf16[4,2,128,1536]{3,2,1,0:T(8,128)(2,1)S(1)} custom-call(s32[2]{0:T(128)S(1)} %fusion.28.lengths_ref, bf16[4,2,128,1536]{3,2,1,0:T(8,128)(2,1)S(1)} %bitcast.160, bf16[4,2,128,1536]{3,2,1,0:T(8,128)(2,1)S(1)} %bitcast.161, bf16[4,2,128,1536]{3,2,1,0:T(8,128)(2,1)S(1)} %bitcast.162, bf16[4,2,128,512]{3,2,1,0:T(8,128)(2,1)S(1)} %bitcast.177, ...), custom_call_target="tpu_custom_call" | custom-call | flops 5368709120 | bytes 7340032 | tf_op jit(solution)/shard_map/pallas_call | solution.py:141
  537.2 6.6 add_convert_fusion.1
  545.6 7.8 %add_convert_fusion.4 = bf16[1024,1024]{1,0:T(8,128)(2,1)} fusion(f32[1024,1024]{1,0:T(8,128)} %copy-done.15, f32[1024,1024]{1,0:T(8,128)} %fusion.40, bf16[1024,1536]{1,0:T(8,128)(2,1)} %bitcast.171, bf16[1024,1536]{1,0:T(8,128)(2,1)S(1)} %copy-done.58), kind=kOutput, calls=%fused_computation.44 | convolution fusion | flops 3224371200 | bytes 16777216 | tf_op jit(solution)/shard_map/dot_general | solution.py:25
  562.3 12.6 %collective-permute-done.26 = bf16[512,512]{1,0:T(8,128)(2,1)S(1)} collective-permute-done((bf16[512,512]{1,0:T(8,128)(2,1)S(1)}, bf16[512,512]{1,0:T(8,128)(2,1)S(1)}, u32[]{:S(2)}, u32[]{:S(2)}) %collective-permute-start.26) | collective-permute-done | bytes 524320 | tf_op jit(solution)/shard_map/ppermute | solution.py:208
  585.3 18.6 %collective-permute-done.31 = f32[8192]{0:T(1024)S(1)} collective-permute-done((f32[8192]{0:T(1024)S(1)}, f32[8192]{0:T(1024)S(1)}, u32[]{:S(2)}, u32[]{:S(2)}) %collective-permute-start.31) | collective-permute-done | bytes 32800 | tf_op jit(solution)/shard_map/ppermute | solution.py:178
  606.8 20.9 %collective-permute-done.32 = f32[8192]{0:T(1024)S(1)} collective-permute-done((f32[8192]{0:T(1024)S(1)}, f32[8192]{0:T(1024)S(1)}, u32[]{:S(2)}, u32[]{:S(2)}) %collective-permute-start.32) | collective-permute-done | bytes 32800 | tf_op jit(solution)/shard_map/ppermute | solution.py:178
  645.0 21.8 %collective-permute-done.22 = f32[1536]{0:T(1024)S(1)} collective-permute-done((f32[1536]{0:T(1024)S(1)}, f32[1536]{0:T(1024)S(1)}, u32[]{:S(2)}, u32[]{:S(2)}) %collective-permute-start.22) | collective-permute-done | bytes 6176 | tf_op jit(solution)/shard_map/ppermute | solution.py:178
  676.3 11.3 %collective-permute-done.36 = bf16[64,2048]{1,0:T(8,128)(2,1)S(1)} collective-permute-done((bf16[64,2048]{1,0:T(8,128)(2,1)S(1)}, bf16[64,2048]{1,0:T(8,128)(2,1)S(1)}, u32[]{:S(2)}, u32[]{:S(2)}) %collective-permute-start.36) | collective-permute-done | bytes 262176 | tf_op jit(solution)/shard_map/ppermute | solution.py:208
  693.1 14.3 %reduce-scatter.5.cloned.1.call-done = bf16[64,1536]{1,0:T(8,128)(2,1)} async-done(((bf16[1024,1536]{1,0:T(8,128)(2,1)}), bf16[64,1536]{1,0:T(8,128)(2,1)}) %reduce-scatter.5.cloned.1.call-update) | async-done | bytes 196624 | tf_op jit(solution)/shard_map/reduce_scatter | solution.py:232
  (319 shorter events, 199.6 us)
Async XLA Ops:
  7.2 134.1 %all-gather.3.cloned.1.call-start = ((), (), s32[]{:S(2)}) async-start(), calls=%async_computation.6 | async-start | bytes 3342336 | tf_op jit(solution)/shard_map/all_gather | solution.py:218
  8.9 263.0 %all-gather.5.cloned.1.call-start = ((), (), s32[]{:S(2)}) async-start(), calls=%async_computation.7 | async-start | bytes 4456448 | tf_op jit(solution)/shard_map/all_gather | solution.py:218
  20.3 42.6 %collective-permute-start.8 = (bf16[128,2048]{1,0:T(8,128)(2,1)S(1)}, bf16[128,2048]{1,0:T(8,128)(2,1)}, u32[]{:S(2)}, u32[]{:S(2)}) collective-permute-start(bf16[128,2048]{1,0:T(8,128)(2,1)S(1)} %pad_maximum_fusion.7), channel_id=1, source_target_pairs={{0,4},{2,6},{4,0},{6,2},{1,5},{3,7},{5,1},{7,3},{8,12},{10,14},{12... | collective-permute-start | bytes 1572872 | tf_op jit(solution)/shard_map/ppermute | solution.py:194
  23.1 16.1 %collective-permute-start = (bf16[64,512]{1,0:T(8,128)(2,1)}, bf16[64,512]{1,0:T(8,128)(2,1)S(1)}, u32[]{:S(2)}, u32[]{:S(2)}) collective-permute-start(bf16[64,512]{1,0:T(8,128)(2,1)} %bitcast.210), channel_id=1, source_target_pairs={{0,2},{2,0},{4,6},{6,4},{1,3},{3,1},{5,7},{7,5},{8,10},{10,8},{12,... | collective-permute-start | bytes 196616 | tf_op jit(solution)/shard_map/ppermute | solution.py:194
  29.1 188.9 %all-to-all-start = ((bf16[4,2,128,1024]{2,3,1,0:T(8,128)(2,1)}), bf16[4,2,128,1024]{2,3,1,0:T(8,128)(2,1)S(1)}, u32[]{:S(2)}, u32[]{:S(2)}) async-start(bf16[4,2,128,1024]{2,3,1,0:T(8,128)(2,1)} %bitcast.184), calls=%async_computation | async-start | bytes 4194304 | tf_op jit(solution)/shard_map/all_to_all | solution.py:265
  65.3 70.7 %collective-permute-start.9 = (bf16[256,2048]{1,0:T(8,128)(2,1)}, bf16[256,2048]{1,0:T(8,128)(2,1)}, u32[]{:S(2)}, u32[]{:S(2)}) collective-permute-start(bf16[256,2048]{1,0:T(8,128)(2,1)} %pad_maximum_fusion.5), channel_id=1, source_target_pairs={{0,8},{8,0},{16,24},{24,16},{1,9},{9,1},{17,25},{25,17},{2,10},{10... | collective-permute-start | bytes 3145736 | tf_op jit(solution)/shard_map/ppermute | solution.py:194
  66.8 58.9 %collective-permute-start.1 = (bf16[128,512]{1,0:T(8,128)(2,1)S(1)}, bf16[128,512]{1,0:T(8,128)(2,1)S(1)}, u32[]{:S(2)}, u32[]{:S(2)}) collective-permute-start(bf16[128,512]{1,0:T(8,128)(2,1)S(1)} %pad_maximum_fusion.9), channel_id=1, source_target_pairs={{0,4},{2,6},{4,0},{6,2},{1,5},{3,7},{5,1},{7,3},{8,12},{10,14},{12... | collective-permute-start | bytes 393224 | tf_op jit(solution)/shard_map/ppermute | solution.py:194
  140.4 94.4 %collective-permute-start.10 = (bf16[512,2048]{1,0:T(8,128)(2,1)}, bf16[512,2048]{1,0:T(8,128)(2,1)}, u32[]{:S(2)}, u32[]{:S(2)}) collective-permute-start(bf16[512,2048]{1,0:T(8,128)(2,1)} %pad_maximum_fusion.3), channel_id=1, source_target_pairs={{0,16},{8,24},{16,0},{24,8},{1,17},{9,25},{17,1},{25,9},{2,18},{10... | collective-permute-start | bytes 6291464 | tf_op jit(solution)/shard_map/ppermute | solution.py:194
  141.3 112.3 %collective-permute-start.4 = (bf16[1024,1536]{1,0:T(8,128)(2,1)}, bf16[1024,1536]{1,0:T(8,128)(2,1)}, u32[]{:S(2)}, u32[]{:S(2)}) collective-permute-start(bf16[1024,1536]{1,0:T(8,128)(2,1)} %all-gather.3.cloned.1.call-done), channel_id=1, source_target_pairs={{0,1},{1,0},{2,3},{3,2},{4,5},{5,4},{6,7},{7,6},{8,9},{9,8},{10,11... | collective-permute-start | bytes 9437192 | tf_op jit(solution)/shard_map/ppermute | solution.py:171
  142.1 74.4 %collective-permute-start.3 = (bf16[512,512]{1,0:T(8,128)(2,1)}, bf16[512,512]{1,0:T(8,128)(2,1)S(1)}, u32[]{:S(2)}, u32[]{:S(2)}) collective-permute-start(bf16[512,512]{1,0:T(8,128)(2,1)} %pad_maximum_fusion.6), channel_id=1, source_target_pairs={{0,16},{8,24},{16,0},{24,8},{1,17},{9,25},{17,1},{25,9},{2,18},{10... | collective-permute-start | bytes 1572872 | tf_op jit(solution)/shard_map/ppermute | solution.py:194
  218.0 54.3 %collective-permute-start.6 = (bf16[1024,512]{1,0:T(8,128)(2,1)}, bf16[1024,512]{1,0:T(8,128)(2,1)}, u32[]{:S(2)}, u32[]{:S(2)}) collective-permute-start(bf16[1024,512]{1,0:T(8,128)(2,1)} %pad_maximum_fusion.4), channel_id=1, source_target_pairs={{0,1},{1,0},{2,3},{3,2},{4,5},{5,4},{6,7},{7,6},{8,9},{9,8},{10,11... | collective-permute-start | bytes 3145736 | tf_op jit(solution)/shard_map/ppermute | solution.py:171
  228.5 55.2 %all-to-all-start.2 = ((bf16[4,2,128,1024]{3,2,1,0:T(8,128)(2,1)}), bf16[4,2,128,1024]{3,2,1,0:T(8,128)(2,1)}, u32[]{:S(2)}, u32[]{:S(2)}) async-start(bf16[4,2,128,1024]{3,2,1,0:T(8,128)(2,1)} %dynamic-slice_bitcast_fusion), calls=%async_computation.2 | async-start | bytes 4194304 | tf_op jit(solution)/shard_map/all_to_all | solution.py:265
  271.8 32.0 %collective-permute-start.11 = (bf16[1024,2048]{1,0:T(8,128)(2,1)}, bf16[1024,2048]{1,0:T(8,128)(2,1)}, u32[]{:S(2)}, u32[]{:S(2)}) collective-permute-start(bf16[1024,2048]{1,0:T(8,128)(2,1)} %all-gather.5.cloned.1.call-done), channel_id=1, source_target_pairs={{0,1},{1,0},{2,3},{3,2},{4,5},{5,4},{6,7},{7,6},{8,9},{9,8},{10,11... | collective-permute-start | bytes 12582920 | tf_op jit(solution)/shard_map/ppermute | solution.py:171
  272.0 40.8 %collective-permute-start.12 = (bf16[1024,2048]{1,0:T(8,128)(2,1)}, bf16[1024,2048]{1,0:T(8,128)(2,1)}, u32[]{:S(2)}, u32[]{:S(2)}) collective-permute-start(bf16[1024,2048]{1,0:T(8,128)(2,1)} %pad_maximum_fusion), channel_id=1, source_target_pairs={{0,1},{1,0},{2,3},{3,2},{4,5},{5,4},{6,7},{7,6},{8,9},{9,8},{10,11... | collective-permute-start | bytes 12582920 | tf_op jit(solution)/shard_map/ppermute | solution.py:171
  332.0 83.8 %all-to-all-start.1 = ((bf16[4,2,128,1024]{3,2,1,0:T(8,128)(2,1)}), bf16[4,2,128,1024]{3,2,1,0:T(8,128)(2,1)}, u32[]{:S(2)}, u32[]{:S(2)}) async-start(bf16[4,2,128,1024]{3,2,1,0:T(8,128)(2,1)} %bitcast.183), calls=%async_computation.1 | async-start | bytes 4194304 | tf_op jit(solution)/shard_map/all_to_all | solution.py:270
  336.5 207.3 %reduce-scatter.3.cloned.1.call-start = ((), (), s32[]{:S(2)}) async-start(), calls=%async_computation.8 | async-start | bytes 4456448 | tf_op jit(solution)/shard_map/reduce_scatter | solution.py:232
  363.1 53.2 %collective-permute-start.14 = (bf16[1024,2048]{1,0:T(8,128)(2,1)}, bf16[1024,2048]{1,0:T(8,128)(2,1)}, u32[]{:S(2)}, u32[]{:S(2)}) collective-permute-start(bf16[1024,2048]{1,0:T(8,128)(2,1)} %convolution_convert_fusion.1), channel_id=1, source_target_pairs={{0,1},{1,0},{2,3},{3,2},{4,5},{5,4},{6,7},{7,6},{8,9},{9,8},{10,11... | collective-permute-start | bytes 12582920 | tf_op jit(solution)/shard_map/ppermute | solution.py:171
  363.1 30.2 %collective-permute-start.17 = (bf16[1024,2048]{1,0:T(8,128)(2,1)}, bf16[1024,2048]{1,0:T(8,128)(2,1)}, u32[]{:S(2)}, u32[]{:S(2)}) collective-permute-start(bf16[1024,2048]{1,0:T(8,128)(2,1)} %convolution_convert_fusion), channel_id=1, source_target_pairs={{0,1},{1,0},{2,3},{3,2},{4,5},{5,4},{6,7},{7,6},{8,9},{9,8},{10,11... | collective-permute-start | bytes 12582920 | tf_op jit(solution)/shard_map/ppermute | solution.py:171
  401.2 306.2 %reduce-scatter.5.cloned.1.call-start = ((), (), s32[]{:S(2)}) async-start(), calls=%async_computation.9 | async-start | bytes 3342336 | tf_op jit(solution)/shard_map/reduce_scatter | solution.py:232
  410.1 148.4 %collective-permute-start.25 = (bf16[1024,512]{1,0:T(8,128)(2,1)}, bf16[1024,512]{1,0:T(8,128)(2,1)}, u32[]{:S(2)}, u32[]{:S(2)}) collective-permute-start(bf16[1024,512]{1,0:T(8,128)(2,1)} %convolution_convert_fusion.2), channel_id=1, source_target_pairs={{0,1},{1,0},{2,3},{3,2},{4,5},{5,4},{6,7},{7,6},{8,9},{9,8},{10,11... | collective-permute-start | bytes 3145736 | tf_op jit(solution)/shard_map/ppermute | solution.py:171
  415.8 111.3 %collective-permute-start.13 = (bf16[4,2,128,1024]{3,2,1,0:T(8,128)(2,1)}, bf16[4,2,128,1024]{3,2,1,0:T(8,128)(2,1)}, u32[]{:S(2)}, u32[]{:S(2)}) collective-permute-start(bf16[4,2,128,1024]{3,2,1,0:T(8,128)(2,1)} %all-to-all-done.1), channel_id=1, source_target_pairs={{0,1},{1,0},{2,3},{3,2},{4,5},{5,4},{6,7},{7,6},{8,9},{9,8},{10,11... | collective-permute-start | bytes 6291464 | tf_op jit(solution)/shard_map/ppermute | solution.py:171
  425.4 82.9 %collective-permute-start.15 = (bf16[512,2048]{1,0:T(8,128)(2,1)S(1)}, bf16[512,2048]{1,0:T(8,128)(2,1)}, u32[]{:S(2)}, u32[]{:S(2)}) collective-permute-start(bf16[512,2048]{1,0:T(8,128)(2,1)S(1)} %fusion.18), channel_id=1, source_target_pairs={{0,16},{8,24},{16,0},{24,8},{1,17},{9,25},{17,1},{25,9},{2,18},{10... | collective-permute-start | bytes 6291464 | tf_op jit(solution)/shard_map/ppermute | solution.py:208
  448.2 89.0 %collective-permute-start.19 = (bf16[1024,1536]{1,0:T(8,128)(2,1)}, bf16[1024,1536]{1,0:T(8,128)(2,1)}, u32[]{:S(2)}, u32[]{:S(2)}) collective-permute-start(bf16[1024,1536]{1,0:T(8,128)(2,1)} %bitcast_convert_fusion), channel_id=1, source_target_pairs={{0,1},{1,0},{2,3},{3,2},{4,5},{5,4},{6,7},{7,6},{8,9},{9,8},{10,11... | collective-permute-start | bytes 9437192 | tf_op jit(solution)/shard_map/ppermute | solution.py:171
  510.8 24.7 %collective-permute-start.16 = (bf16[256,2048]{1,0:T(8,128)(2,1)S(1)}, bf16[256,2048]{1,0:T(8,128)(2,1)S(1)}, u32[]{:S(2)}, u32[]{:S(2)}) collective-permute-start(bf16[256,2048]{1,0:T(8,128)(2,1)S(1)} %fusion.19), channel_id=1, source_target_pairs={{0,8},{8,0},{16,24},{24,16},{1,9},{9,1},{17,25},{25,17},{2,10},{10... | collective-permute-start | bytes 3145736 | tf_op jit(solution)/shard_map/ppermute | solution.py:208
  553.4 85.2 %all-to-all-start.3 = ((bf16[4,2,128,1024]{3,2,1,0:T(8,128)(2,1)}), bf16[4,2,128,1024]{3,2,1,0:T(8,128)(2,1)}, u32[]{:S(2)}, u32[]{:S(2)}) async-start(bf16[4,2,128,1024]{3,2,1,0:T(8,128)(2,1)} %bitcast.198), calls=%async_computation.3 | async-start | bytes 4194304 | tf_op jit(solution)/shard_map/all_to_all | solution.py:270
  577.5 26.5 %collective-permute-start.31 = (f32[8192]{0:T(1024)S(1)}, f32[8192]{0:T(1024)S(1)}, u32[]{:S(2)}, u32[]{:S(2)}) collective-permute-start(f32[8192]{0:T(1024)S(1)} %add.327), channel_id=1, source_target_pairs={{0,2},{2,0},{4,6},{6,4},{1,3},{3,1},{5,7},{7,5},{8,10},{10,8},{12,... | collective-permute-start | bytes 98312 | tf_op jit(solution)/shard_map/ppermute | solution.py:178
  582.5 53.3 %collective-permute-start.28 = (bf16[128,512]{1,0:T(8,128)(2,1)S(1)}, bf16[128,512]{1,0:T(8,128)(2,1)}, u32[]{:S(2)}, u32[]{:S(2)}) collective-permute-start(bf16[128,512]{1,0:T(8,128)(2,1)S(1)} %fusion.25), channel_id=1, source_target_pairs={{0,4},{2,6},{4,0},{6,2},{1,5},{3,7},{5,1},{7,3},{8,12},{10,14},{12... | collective-permute-start | bytes 393224 | tf_op jit(solution)/shard_map/ppermute | solution.py:208
  604.0 23.8 %collective-permute-start.32 = (f32[8192]{0:T(1024)S(1)}, f32[8192]{0:T(1024)S(1)}, u32[]{:S(2)}, u32[]{:S(2)}) collective-permute-start(f32[8192]{0:T(1024)S(1)} %add.328), channel_id=1, source_target_pairs={{0,4},{2,6},{4,0},{6,2},{1,5},{3,7},{5,1},{7,3},{8,12},{10,14},{12... | collective-permute-start | bytes 98312 | tf_op jit(solution)/shard_map/ppermute | solution.py:178
  638.6 49.8 %collective-permute-start.18 = (bf16[4,2,128,1024]{3,2,1,0:T(8,128)(2,1)}, bf16[4,2,128,1024]{3,2,1,0:T(8,128)(2,1)S(1)}, u32[]{:S(2)}, u32[]{:S(2)}) collective-permute-start(bf16[4,2,128,1024]{3,2,1,0:T(8,128)(2,1)} %all-to-all-done.3), channel_id=1, source_target_pairs={{0,1},{1,0},{2,3},{3,2},{4,5},{5,4},{6,7},{7,6},{8,9},{9,8},{10,11... | collective-permute-start | bytes 6291464 | tf_op jit(solution)/shard_map/ppermute | solution.py:171
  640.1 34.1 %collective-permute-start.35 = (bf16[128,2048]{1,0:T(8,128)(2,1)S(1)}, bf16[128,2048]{1,0:T(8,128)(2,1)S(1)}, u32[]{:S(2)}, u32[]{:S(2)}) collective-permute-start(bf16[128,2048]{1,0:T(8,128)(2,1)S(1)} %fusion.21), channel_id=1, source_target_pairs={{0,4},{2,6},{4,0},{6,2},{1,5},{3,7},{5,1},{7,3},{8,12},{10,14},{12... | collective-permute-start | bytes 1572872 | tf_op jit(solution)/shard_map/ppermute | solution.py:208
  642.2 24.6 %collective-permute-start.22 = (f32[1536]{0:T(1024)S(1)}, f32[1536]{0:T(1024)S(1)}, u32[]{:S(2)}, u32[]{:S(2)}) collective-permute-start(f32[1536]{0:T(1024)S(1)} %add.314), channel_id=1, source_target_pairs={{0,4},{2,6},{4,0},{6,2},{1,5},{3,7},{5,1},{7,3},{8,12},{10,14},{12... | collective-permute-start | bytes 18440 | tf_op jit(solution)/shard_map/ppermute | solution.py:178
  643.1 28.7 %collective-permute-start.29 = (bf16[64,512]{1,0:T(8,128)(2,1)S(1)}, bf16[64,512]{1,0:T(8,128)(2,1)S(1)}, u32[]{:S(2)}, u32[]{:S(2)}) collective-permute-start(bf16[64,512]{1,0:T(8,128)(2,1)S(1)} %fusion.27), channel_id=1, source_target_pairs={{0,2},{2,0},{4,6},{6,4},{1,3},{3,1},{5,7},{7,5},{8,10},{10,8},{12,... | collective-permute-start | bytes 196616 | tf_op jit(solution)/shard_map/ppermute | solution.py:208
  (80 other events, 704.1 us)
Sparse Core Ops, SparseCore 0:
  11.4 113.8 all-gather.2
  128.1 93.2 all-gather.4
  401.4 97.7 reduce-scatter.2
  545.7 161.6 reduce-scatter.4
